TPU v7x, 32 devices: a whole 2x2x4 slice. The times are simulated.
32 devices in a mesh: groups: 2 (over x), dp: 16 (over z, y, core).
Axes of the slice: x: 2, y: 2, z: 4, core: 2. Of those that a mesh axis runs over, the one named last changes fastest.
Arguments:
- acts: bfloat16 [12288, 8192], P(('groups', 'dp')), parts along dimension 0, may hold values from -6 to 6
- grad_out: bfloat16 [12288, 1024], P(('groups', 'dp')), parts along dimension 0, may hold values from -0.29882812 to 0.29882812
- low_acts: bfloat16 [12288, 64], P(('groups', 'dp')), parts along dimension 0, may hold values from -6 to 6
- up_weight: bfloat16 [64, 64, 1024], P('dp'), may hold values from -0.1875 to 0.1875
- block_adapter: int32 [96], P('groups'), parts along dimension 0, may hold values from 0 to 63
- block_fill: int32 [96], P(('groups', 'dp')), parts along dimension 0, may hold values from 32 to 128
- owner_slot: int32 [64], replicated, may hold values from 0 to 63, each once
Outputs:
- grad_down: bfloat16 [128, 64, 8192], P(('groups', 'dp')), parts along dimension 0
- grad_up: bfloat16 [128, 64, 1024], P(('groups', 'dp')), parts along dimension 0
There are 2 independent parts, one for each index of `groups`. A program takes and returns all parts, laid end to end along the dimension named above; an argument that names none is the same for every part. Nothing has to cross between parts.
All inputs are finite; a program needn't handle non-finite values.
Results may differ from a plain program's by a relative error of at most 0.0049.
Values may be sent and summed in bfloat16 or wider, within the bound.
No kernel may reach another device: no remote copies, remote signals or barrier semaphores. Data moves between devices by JAX's collectives and lax.ppermute only.
A program may use at most 128 MiB of HBM per device.

v0:
```python
import jax
import jax.numpy as jnp
from jax import lax
from jax.sharding import PartitionSpec as P

BLOCK = 128


adapter_scale_factor = 2.0


def body(acts, grad_out, low_acts, up_weight, block_adapter, block_fill, owner_slot):
    num_blocks = block_fill.shape[0]
    adapters = owner_slot.shape[0]
    rank_width = low_acts.shape[1]
    adapter_ids = jnp.arange(adapters, dtype=jnp.int32)
    slot_of = jnp.sum(
        jnp.where(block_adapter[:, None] == adapter_ids[None, :], owner_slot[None, :], 0), axis=1
    )
    slot_hot = (slot_of[:, None] == adapter_ids[None, :]).astype(jnp.bfloat16)
    positions = jnp.arange(BLOCK, dtype=jnp.int32)
    live = (positions[None, :] < block_fill[:, None]).astype(jnp.bfloat16)
    masked_gradient = grad_out.reshape(num_blocks, BLOCK, -1) * live[:, :, None]
    up_cols = lax.all_to_all(up_weight, "dp", split_axis=2, concat_axis=0, tiled=True)
    up_picked = jnp.einsum(
        "bs,sro->bro", slot_hot, up_cols, preferred_element_type=jnp.float32
    ).astype(jnp.bfloat16)
    owned_up_gradient = lax.all_to_all(up_picked, "dp", split_axis=0, concat_axis=2, tiled=True)
    reduced_rank_gradient = (
        adapter_scale_factor
        * jnp.einsum(
            "iye,iwe->iyw", masked_gradient, owned_up_gradient, preferred_element_type=jnp.float32
        )
    ).astype(jnp.bfloat16)
    flat_masked = masked_gradient.reshape(num_blocks * BLOCK, -1)
    rows_act, rows_grad = (
        lax.all_to_all(acts, "dp", split_axis=1, concat_axis=0, tiled=True),
        lax.all_to_all(flat_masked, "dp", split_axis=1, concat_axis=0, tiled=True),
    )
    all_low_grad, all_low = (
        lax.all_gather(
            reduced_rank_gradient.reshape(num_blocks * BLOCK, rank_width), "dp", axis=0, tiled=True
        ),
        lax.all_gather(low_acts, "dp", axis=0, tiled=True),
    )
    total_blocks = rows_act.shape[0] // BLOCK
    got_down = jnp.einsum(
        "gif,gil->gfl",
        all_low_grad.reshape(total_blocks, BLOCK, rank_width),
        rows_act.reshape(total_blocks, BLOCK, -1),
        preferred_element_type=jnp.float32,
    )
    received_up_gradient = adapter_scale_factor * jnp.einsum(
        "bkr,bko->bro",
        all_low.reshape(total_blocks, BLOCK, rank_width),
        rows_grad.reshape(total_blocks, BLOCK, -1),
        preferred_element_type=jnp.float32,
    )
    sum_down = jax.ops.segment_sum(got_down, slot_of, num_segments=adapters).astype(jnp.bfloat16)
    sum_up = jax.ops.segment_sum(received_up_gradient, slot_of, num_segments=adapters).astype(
        jnp.bfloat16
    )
    own_down, own_upgrad = (
        lax.all_to_all(sum_down, "dp", split_axis=0, concat_axis=2, tiled=True),
        lax.all_to_all(sum_up, "dp", split_axis=0, concat_axis=2, tiled=True),
    )
    return (own_down, own_upgrad)


def solution(mesh):
    placed = (
        P(("groups", "dp"), None),
        P(("groups", "dp"), None),
        P(("groups", "dp"), None),
        P("dp", None, None),
        P("groups"),
        P(("groups", "dp")),
        P(),
    )
    return jax.shard_map(
        body,
        mesh=mesh,
        in_specs=placed,
        out_specs=(P(("groups", "dp"), None, None), P(("groups", "dp"), None, None)),
        check_vma=False,
    )
```

profile of v0, /device:TPU:15, one launch (start us, length us, event | category | flops | bytes accessed | tf_op | source)
XLA Modules:
  0.0 399.7 jit_solution(16334576864036602608)
XLA Ops:
  0.7 1.7 copy.53
  3.9 6.6 %all-to-all-start = ((bf16[16,2,8192]{2,1,0:T(2,128)(2,1)}), bf16[16,2,8192]{2,1,0:T(2,128)(2,1)S(1)}, u32[]{:S(2)}, u32[]{:S(2)}) async-start(bf16[16,2,8192]{2,1,0:T(2,128)(2,1)} %reshape.89), calls=%async_computation | async-start | bytes 1048576 | tf_op jit(solution)/shard_map/all_to_all | solution.py:24
  11.8 12.2 %all-to-all-done = bf16[16,2,8192]{2,1,0:T(2,128)(2,1)S(1)} async-done(((bf16[16,2,8192]{2,1,0:T(2,128)(2,1)}), bf16[16,2,8192]{2,1,0:T(2,128)(2,1)S(1)}, u32[]{:S(2)}, u32[]{:S(2)}) %all-to-all-start) | async-done | bytes 524320 | tf_op jit(solution)/shard_map/all_to_all | solution.py:24
  24.0 5.0 %all-to-all-start.4 = ((bf16[384,16,64]{0,2,1:T(8,128)(2,1)}), bf16[384,16,64]{0,2,1:T(8,128)(2,1)S(1)}, u32[]{:S(2)}, u32[]{:S(2)}) async-start(bf16[384,16,64]{0,2,1:T(8,128)(2,1)} %bitcast.12), calls=%async_computation.4 | async-start | bytes 1572864 | tf_op jit(solution)/shard_map/all_to_all | solution.py:38
  29.9 1.8 copy.54
  33.6 14.6 %all-to-all-done.4 = bf16[384,16,64]{0,2,1:T(8,128)(2,1)S(1)} async-done(((bf16[384,16,64]{0,2,1:T(8,128)(2,1)}), bf16[384,16,64]{0,2,1:T(8,128)(2,1)S(1)}, u32[]{:S(2)}, u32[]{:S(2)}) %all-to-all-start.4) | async-done | bytes 786464 | tf_op jit(solution)/shard_map/all_to_all | solution.py:38
  48.2 5.0 %all-to-all-start.1 = ((bf16[16,2,6144]{2,1,0:T(2,128)(2,1)}), bf16[16,2,6144]{2,1,0:T(2,128)(2,1)S(1)}, u32[]{:S(2)}, u32[]{:S(2)}) async-start(bf16[16,2,6144]{2,1,0:T(2,128)(2,1)} %reshape.91), calls=%async_computation.1 | async-start | bytes 786432 | tf_op jit(solution)/shard_map/all_to_all | solution.py:28
  53.2 6.1 %copy.84 = bf16[48,16,8,512]{3,2,0,1:T(8,128)(2,1)} copy(bf16[48,16,8,512]{3,2,1,0:T(8,128)(2,1)} %bitcast.63) | data formatting | bytes 12582912 | tf_op jit(solution)/shard_map/all_to_all | solution.py:37
  59.3 4.7 %all-to-all-done.1 = bf16[16,2,6144]{2,1,0:T(2,128)(2,1)S(1)} async-done(((bf16[16,2,6144]{2,1,0:T(2,128)(2,1)}), bf16[16,2,6144]{2,1,0:T(2,128)(2,1)S(1)}, u32[]{:S(2)}, u32[]{:S(2)}) %all-to-all-start.1) | async-done | bytes 393248 | tf_op jit(solution)/shard_map/all_to_all | solution.py:28
  63.9 6.1 %all-to-all-start.2 = ((bf16[384,16,512]{2,0,1:T(8,128)(2,1)}), bf16[384,16,512]{2,0,1:T(8,128)(2,1)}, u32[]{:S(2)}, u32[]{:S(2)}) async-start(bf16[384,16,512]{2,0,1:T(8,128)(2,1)} %bitcast.62), calls=%async_computation.2 | async-start | bytes 12582912 | tf_op jit(solution)/shard_map/all_to_all | solution.py:37
  70.0 150.8 %all_gather.7 = bf16[6144,64]{0,1:T(8,128)(2,1)} all-gather(bf16[384,64]{0,1:T(8,128)(2,1)S(1)} %copy-done.1), channel_id=1, replica_groups=mesh['groups'=2,'dp'=16] {'dp'}, dimensions={0}, use_global_device_ids=true | all-gather | bytes 835584 | tf_op jit(solution)/shard_map/all_gather | solution.py:44
  221.6 1.7 multiply_bitcast_fusion
  223.3 1.6 copy.65
  225.1 5.4 %scatter_fusion.1 = f32[64,64,64]{2,1,0:T(8,128)S(1)} fusion(f32[64,64,64]{2,1,0:T(8,128)S(1)} %broadcast_in_dim.34, s32[48]{0:T(128)S(1)} %select_reduce_fusion, f32[48,64,64]{2,1,0:T(8,128)} %copy.65), kind=kCustom, calls=%fused_computation.1 | custom fusion | flops 196608 | bytes 2359488 | tf_op jit(solution)/shard_map/scatter-add | solution.py:60
  233.8 5.1 %all-to-all-start.5 = ((bf16[16,2,8192]{2,1,0:T(2,128)(2,1)}), bf16[16,2,8192]{2,1,0:T(2,128)(2,1)S(1)}, u32[]{:S(2)}, u32[]{:S(2)}) async-start(bf16[16,2,8192]{2,1,0:T(2,128)(2,1)} %reshape.93), calls=%async_computation.5 | async-start | bytes 1048576 | tf_op jit(solution)/shard_map/all_to_all | solution.py:65
  239.0 1.6 fusion.1
  240.6 24.2 %all_gather.6 = bf16[6144,64]{0,1:T(8,128)(2,1)S(1)} all-gather(bf16[384,64]{0,1:T(8,128)(2,1)S(1)} %bitcast.72), channel_id=1, replica_groups=mesh['groups'=2,'dp'=16] {'dp'}, dimensions={0}, use_global_device_ids=true | all-gather | bytes 835584 | tf_op jit(solution)/shard_map/all_gather | solution.py:41
  264.8 6.5 %fusion.4 = f32[48,64,512]{2,1,0:T(8,128)} fusion(bf16[48,128,512]{2,1,0:T(8,128)(2,1)} %bitcast.8, bf16[6144,64]{0,1:T(8,128)(2,1)S(1)} %all_gather.6), kind=kOutput, calls=%fused_computation.10 | convolution fusion | flops 402653184 | bytes 13369344 | tf_op jit(solution)/shard_map/gif,gil->gfl/dot_general | solution.py:47
  271.3 4.3 %broadcast_in_dim.18 = f32[64,64,512]{2,1,0:T(8,128)} broadcast(f32[]{:T(128)} %constant.3.clone.1), dimensions={} | broadcast | bytes 8388612 | tf_op jit(solution)/shard_map/broadcast_in_dim | solution.py:59
  275.6 14.5 %scatter_fusion = f32[64,64,512]{2,1,0:T(8,128)} fusion(f32[64,64,512]{2,1,0:T(8,128)} %broadcast_in_dim.18, s32[48]{0:T(128)S(1)} %select_reduce_fusion, f32[48,64,512]{2,1,0:T(8,128)} %fusion.4), kind=kCustom, calls=%fused_computation | custom fusion | flops 1572864 | bytes 18874560 | tf_op jit(solution)/shard_map/scatter-add | solution.py:59
  290.0 6.0 %convert_element_type.29 = bf16[64,64,512]{2,1,0:T(8,128)(2,1)} convert(f32[64,64,512]{2,1,0:T(8,128)} %scatter_fusion) | non-fusion elementwise | flops 2097152 | bytes 12582912 | tf_op jit(solution)/shard_map/convert_element_type | solution.py:59
  296.1 6.3 %all-to-all-start.3 = ((bf16[64,64,512]{2,1,0:T(8,128)(2,1)}), bf16[64,64,512]{2,1,0:T(8,128)(2,1)}, u32[]{:S(2)}, u32[]{:S(2)}) async-start(bf16[64,64,512]{2,1,0:T(8,128)(2,1)} %convert_element_type.29), calls=%async_computation.3 | async-start | bytes 8388608 | tf_op jit(solution)/shard_map/all_to_all | solution.py:64
  305.3 89.6 %all-to-all-done.3 = bf16[64,64,512]{2,1,0:T(8,128)(2,1)} async-done(((bf16[64,64,512]{2,1,0:T(8,128)(2,1)}), bf16[64,64,512]{2,1,0:T(8,128)(2,1)}, u32[]{:S(2)}, u32[]{:S(2)}) %all-to-all-start.3) | async-done | bytes 4194336 | tf_op jit(solution)/shard_map/all_to_all | solution.py:64
  394.9 4.8 %copy.71 = bf16[16,4,8,8,512]{4,3,0,2,1:T(8,128)(2,1)} copy(bf16[16,4,8,8,512]{4,3,2,1,0:T(8,128)(2,1)} %bitcast.30) | data formatting | bytes 8388608 | tf_op jit(solution)/shard_map/all_to_all | solution.py:64
  (33 shorter events, 12.8 us)
Async XLA Ops:
  0.6 9.8 %copy-start = (bf16[384,1024]{1,0:T(8,128)(2,1)S(1)}, bf16[384,1024]{1,0:T(8,128)(2,1)}, u32[]{:S(2)}) copy-start(bf16[384,1024]{1,0:T(8,128)(2,1)} %param.8) | copy-start | bytes 2359300
  0.6 10.1 %copy-start.2 = (s32[3]{0:T(128)S(1)}, s32[3]{0:T(128)}, u32[]{:S(2)}) copy-start(s32[3]{0:T(128)} %param.12) | copy-start | bytes 40
  0.7 28.3 %copy-start.4 = (s32[48]{0:T(128)S(1)}, s32[48]{0:T(128)}, u32[]{:S(2)}) copy-start(s32[48]{0:T(128)} %param.11) | copy-start | bytes 580
  0.7 28.3 %copy-start.3 = (s32[64]{0:T(128)S(1)}, s32[64]{0:T(128)}, u32[]{:S(2)}) copy-start(s32[64]{0:T(128)} %param.13) | copy-start | bytes 772
  3.9 20.1 %all-to-all-start = ((bf16[16,2,8192]{2,1,0:T(2,128)(2,1)}), bf16[16,2,8192]{2,1,0:T(2,128)(2,1)S(1)}, u32[]{:S(2)}, u32[]{:S(2)}) async-start(bf16[16,2,8192]{2,1,0:T(2,128)(2,1)} %reshape.89), calls=%async_computation | async-start | bytes 1048576 | tf_op jit(solution)/shard_map/all_to_all | solution.py:24
  24.0 24.2 %all-to-all-start.4 = ((bf16[384,16,64]{0,2,1:T(8,128)(2,1)}), bf16[384,16,64]{0,2,1:T(8,128)(2,1)S(1)}, u32[]{:S(2)}, u32[]{:S(2)}) async-start(bf16[384,16,64]{0,2,1:T(8,128)(2,1)} %bitcast.12), calls=%async_computation.4 | async-start | bytes 1572864 | tf_op jit(solution)/shard_map/all_to_all | solution.py:38
  48.2 15.7 %all-to-all-start.1 = ((bf16[16,2,6144]{2,1,0:T(2,128)(2,1)}), bf16[16,2,6144]{2,1,0:T(2,128)(2,1)S(1)}, u32[]{:S(2)}, u32[]{:S(2)}) async-start(bf16[16,2,6144]{2,1,0:T(2,128)(2,1)} %reshape.91), calls=%async_computation.1 | async-start | bytes 786432 | tf_op jit(solution)/shard_map/all_to_all | solution.py:28
  63.9 6.1 %copy-start.1 = (bf16[384,64]{0,1:T(8,128)(2,1)S(1)}, bf16[384,64]{0,1:T(8,128)(2,1)}, u32[]{:S(2)}) copy-start(bf16[384,64]{0,1:T(8,128)(2,1)} %param.9) | copy-start | bytes 147460
  63.9 169.9 %all-to-all-start.2 = ((bf16[384,16,512]{2,0,1:T(8,128)(2,1)}), bf16[384,16,512]{2,0,1:T(8,128)(2,1)}, u32[]{:S(2)}, u32[]{:S(2)}) async-start(bf16[384,16,512]{2,0,1:T(8,128)(2,1)} %bitcast.62), calls=%async_computation.2 | async-start | bytes 12582912 | tf_op jit(solution)/shard_map/all_to_all | solution.py:37
  233.8 62.3 %all-to-all-start.5 = ((bf16[16,2,8192]{2,1,0:T(2,128)(2,1)}), bf16[16,2,8192]{2,1,0:T(2,128)(2,1)S(1)}, u32[]{:S(2)}, u32[]{:S(2)}) async-start(bf16[16,2,8192]{2,1,0:T(2,128)(2,1)} %reshape.93), calls=%async_computation.5 | async-start | bytes 1048576 | tf_op jit(solution)/shard_map/all_to_all | solution.py:65
  296.1 98.8 %all-to-all-start.3 = ((bf16[64,64,512]{2,1,0:T(8,128)(2,1)}), bf16[64,64,512]{2,1,0:T(8,128)(2,1)}, u32[]{:S(2)}, u32[]{:S(2)}) async-start(bf16[64,64,512]{2,1,0:T(8,128)(2,1)} %convert_element_type.29), calls=%async_computation.3 | async-start | bytes 8388608 | tf_op jit(solution)/shard_map/all_to_all | solution.py:64
where the time goes:
time: 401 us; the launch traced here: 400 us
  blocking collectives  175 us (44%)
  waiting for transfers between devices  121 us (30%)
  starting transfers between devices  34 us (8%)
  local copies, waits for them, and re-layouts  31.3 us (8%)
  other arithmetic  27.3 us (7%)
  matrix products  10.1 us (3%)
    all_gather x1, blocking collectives, body(): lax.all_gather(low_acts, 'dp', axis=0, tiled=True)  151 us
    all_to_all x1, waiting for transfers between devices, body(): lax.all_to_all(sum_down, 'dp', split_axis=0, concat_axis=2, tiled=True)  89.6 us
    all_gather x1, blocking collectives, body(): lax.all_gather(reduced_rank_gradient.reshape(num_blocks * BLOCK, rank_wid...  24.2 us
    all_to_all x1, waiting for transfers between devices, body(): lax.all_to_all(flat_masked, 'dp', split_axis=1, concat_axis=0, tiled=True)  14.6 us
    scatter-add x1, other arithmetic, body(): jax.ops.segment_sum(got_down, slot_of, num_segments=adapters)  14.5 us
    all_to_all x1, waiting for transfers between devices, body(): lax.all_to_all(up_weight, 'dp', split_axis=2, concat_axis=0, tiled=True)  12.2 us
    unnamed x18, local copies, waits for them, and re-layouts  8.18 us
  transfers between devices with their start and end apart: 6, of which 4 were waited for; matrix products, arithmetic and copies ran while one was open for 15% of the time, Pallas kernels for 0%

commit v1 on v0

v1 whole, which is shorter than its diff:
```python
import functools

import jax
import jax.numpy as jnp
from jax import lax
from jax.experimental import pallas as pl
from jax.experimental.pallas import tpu as pltpu
from jax.sharding import PartitionSpec as P

BLOCK = 128
SCALE = 2.0
CHUNKS = 2
BF16 = jnp.bfloat16
F32 = jnp.float32
VMEM_LIMIT = 48 * 1024 * 1024


def params():
    return pltpu.CompilerParams(vmem_limit_bytes=VMEM_LIMIT)


def spec():
    return pl.BlockSpec(memory_space=pltpu.VMEM)


def pick_kernel(slot_ref, parts_ref, out_ref):
    def step(b, carry):
        out_ref[b] = parts_ref[slot_ref[b]]
        return carry

    lax.fori_loop(0, out_ref.shape[0], step, 0)


def pick(slot_of, parts):
    blocks = slot_of.shape[0]
    return pl.pallas_call(
        pick_kernel,
        out_shape=jax.ShapeDtypeStruct((blocks,) + parts.shape[1:], BF16),
        in_specs=[pl.BlockSpec(memory_space=pltpu.SMEM), spec()],
        out_specs=spec(),
        compiler_params=params(),
    )(slot_of, parts)


def low_kernel(lane_groups, fill_ref, parts_ref, grad_ref, out_ref, weight):
    parts, blocks, rows, lanes = parts_ref.shape
    for b in range(blocks):
        for p in range(parts):
            g, l = p // lane_groups, p % lane_groups
            weight[b, g * rows : (g + 1) * rows, l * lanes : (l + 1) * lanes] = parts_ref[p, b]
    for b in range(blocks):
        low = SCALE * lax.dot_general(
            weight[b],
            grad_ref[b * BLOCK : (b + 1) * BLOCK, :],
            (((1,), (1,)), ((), ())),
            preferred_element_type=F32,
        )
        live = lax.broadcasted_iota(jnp.int32, low.shape, 1) < fill_ref[b]
        out_ref[b] = jnp.where(live, low, 0.0).astype(BF16)


def rank_cotangent(fill, parts, grad, lane_groups, rank):
    blocks = fill.shape[0]
    return pl.pallas_call(
        functools.partial(low_kernel, lane_groups),
        out_shape=jax.ShapeDtypeStruct((blocks, rank, BLOCK), BF16),
        in_specs=[pl.BlockSpec(memory_space=pltpu.SMEM), spec(), spec()],
        out_specs=spec(),
        scratch_shapes=[pltpu.VMEM((blocks, rank, grad.shape[1]), BF16)],
        compiler_params=params(),
    )(fill, parts, grad)


def up_kernel(fill_ref, low_ref, grad_ref, out_ref):
    parts, blocks, rank, width = out_ref.shape
    for b in range(blocks):
        low = low_ref[:, b * BLOCK : (b + 1) * BLOCK].astype(F32)
        live = lax.broadcasted_iota(jnp.int32, low.shape, 1) < fill_ref[b]
        low = jnp.where(live, low, 0.0).astype(BF16)
        whole = SCALE * jnp.dot(
            low, grad_ref[b * BLOCK : (b + 1) * BLOCK, :], preferred_element_type=F32
        )
        for p in range(parts):
            out_ref[p, b] = whole[:, p * width : (p + 1) * width].astype(BF16)


def up_products(fill, low_t, grad, parts):
    blocks, rank = fill.shape[0], low_t.shape[0]
    return pl.pallas_call(
        up_kernel,
        out_shape=jax.ShapeDtypeStruct((parts, blocks, rank, grad.shape[1] // parts), BF16),
        in_specs=[pl.BlockSpec(memory_space=pltpu.SMEM), spec(), spec()],
        out_specs=spec(),
        compiler_params=params(),
    )(fill, low_t, grad)


def down_kernel(low_ref, acts_ref, out_ref):
    for b in range(low_ref.shape[0]):
        out_ref[0, b] = jnp.dot(
            low_ref[b], acts_ref[b * BLOCK : (b + 1) * BLOCK, :], preferred_element_type=F32
        ).astype(BF16)


def down_products(low_t, acts, parts, chunk):
    blocks, rank, _ = low_t.shape
    rows, width = acts.shape[0], acts.shape[1] // (parts * CHUNKS)
    return pl.pallas_call(
        down_kernel,
        grid=(parts,),
        out_shape=jax.ShapeDtypeStruct((parts, blocks, rank, width), BF16),
        in_specs=[
            pl.BlockSpec(low_t.shape, lambda p: (0, 0, 0)),
            pl.BlockSpec((rows, width), lambda p: (0, chunk * parts + p)),
        ],
        out_specs=pl.BlockSpec((1, blocks, rank, width), lambda p: (p, 0, 0, 0)),
        compiler_params=params(),
        cost_estimate=pl.CostEstimate(
            flops=2 * rows * rank * width * parts,
            bytes_accessed=2 * parts * width * (rows + blocks * rank),
            transcendentals=0,
        ),
    )(low_t, acts)


def sum_kernel(blocks, targets, table_ref, held_ref, *refs):
    extra_ref, out_ref = refs if len(refs) == 2 else (None, refs[0])
    first, last = blocks, blocks + targets

    def step(t, carry):
        def add(j, total):
            return total + held_ref[table_ref[j]].astype(F32)

        total = lax.fori_loop(
            table_ref[first + t], table_ref[last + t], add, jnp.zeros(out_ref.shape[1:], F32)
        )
        if extra_ref is not None:
            place = last + targets

            def add_extra(j, total):
                return total + extra_ref[j].astype(F32)

            total = lax.fori_loop(
                table_ref[place + t], table_ref[place + targets + t], add_extra, total
            )
        out_ref[t] = total.astype(BF16)
        return carry

    lax.fori_loop(0, targets, step, 0)


def slot_sums(table, held, targets, extra=None):
    operands = (held,) if extra is None else (held, extra)
    size = held.shape[1] * held.shape[2]
    moved = 2 * size * (targets + sum(x.shape[0] for x in operands))
    return pl.pallas_call(
        functools.partial(sum_kernel, held.shape[0], targets),
        out_shape=jax.ShapeDtypeStruct((targets,) + held.shape[1:], BF16),
        in_specs=[pl.BlockSpec(memory_space=pltpu.SMEM)] + [spec()] * len(operands),
        out_specs=spec(),
        compiler_params=params(),
        cost_estimate=pl.CostEstimate(
            flops=size * held.shape[0], bytes_accessed=moved, transcendentals=0
        ),
    )(table, *operands)


def place_kernel(got_ref, *refs):
    refs[-1][...] = got_ref[0]


def place(got, columns, chunk, into=None):
    parts, slots, rank, width = got.shape
    return pl.pallas_call(
        place_kernel,
        grid=(parts,),
        out_shape=jax.ShapeDtypeStruct((slots, rank, columns), BF16),
        in_specs=[pl.BlockSpec((1, slots, rank, width), lambda p: (p, 0, 0, 0))]
        + ([] if into is None else [pl.BlockSpec(memory_space=pl.ANY)]),
        out_specs=pl.BlockSpec((slots, rank, width), lambda p: (0, 0, chunk * parts + p)),
        input_output_aliases={} if into is None else {1: 0},
        compiler_params=params(),
        cost_estimate=pl.CostEstimate(
            flops=0, bytes_accessed=4 * parts * slots * rank * width, transcendentals=0
        ),
    )(*((got,) if into is None else (got, into)))


def body(devices, acts, grad_out, low_acts, up_weight, block_adapter, block_fill, owner_slot):
    own_blocks = block_fill.shape[0]
    blocks, adapters = block_adapter.shape[0], owner_slot.shape[0]
    own_slots, rank, out_width = up_weight.shape
    model_width = acts.shape[1]
    half_devices = devices // 2
    half_blocks, half_slots = blocks // 2, adapters // 2
    groups = [list(range(half_devices)), list(range(half_devices, devices))]
    across = [(i, (i + half_devices) % devices) for i in range(devices)]
    half = lax.axis_index("dp") // half_devices

    def within(x):
        return lax.all_to_all(x, "dp", 0, 0, axis_index_groups=groups, tiled=True)

    ids = jnp.arange(adapters, dtype=jnp.int32)
    slot_of = jnp.sum(
        jnp.where(block_adapter[:, None] == ids[None, :], owner_slot[None, :], 0), axis=1
    )

    lane_groups = min(devices // 4, out_width // 128)
    row_groups = devices // lane_groups
    rows, lanes = rank // row_groups, out_width // lane_groups
    pieces = up_weight.reshape(own_slots, row_groups, rows, lane_groups, lanes)
    pieces = pieces.transpose(1, 3, 0, 2, 4).reshape(devices, own_slots, rows, lanes)
    part = lax.all_to_all(pieces, "dp", 0, 0, tiled=True).reshape(adapters, rows, lanes)
    picked = pick(slot_of, part).reshape(devices, own_blocks, rows, lanes)
    weights = lax.all_to_all(picked, "dp", 0, 0, tiled=True)

    up_held = within(up_products(block_fill, low_acts.T, grad_out, half_devices))
    up_held = up_held.reshape(half_blocks, rank, -1)

    mine = lax.dynamic_slice_in_dim(slot_of, half * half_blocks, half_blocks)
    spots = jnp.arange(half_blocks, dtype=jnp.int32)
    before = (mine[None, :] < mine[:, None]) | (
        (mine[None, :] == mine[:, None]) & (spots[None, :] < spots[:, None])
    )
    spot_of = jnp.sum(before.astype(jnp.int32), axis=1)
    order = jnp.sum(jnp.where(spot_of[None, :] == spots[:, None], spots[None, :], 0), axis=1)
    start = jnp.sum((mine[None, :] < ids[:, None]).astype(jnp.int32), axis=1)
    count = jnp.sum((mine[None, :] == ids[:, None]).astype(jnp.int32), axis=1)
    by_half = slot_of.reshape(2, half_blocks)
    has = jnp.any(by_half[:, :, None] == ids[None, None, :], axis=1)
    crosses = has & ((ids[None, :] // half_slots) != jnp.arange(2, dtype=jnp.int32)[:, None])
    earlier = (ids[None, :] < ids[:, None])[None, :, :]
    place_of = jnp.sum((crosses[:, None, :] & earlier).astype(jnp.int32), axis=2)
    needed = lax.pmax(jnp.max(jnp.sum(crosses.astype(jnp.int32), axis=1)), "groups")

    my_cross = lax.dynamic_index_in_dim(crosses, half, 0, False)
    my_place = lax.dynamic_index_in_dim(place_of, half, 0, False)
    hot = my_cross[None, :] & (my_place[None, :] == spots[:, None])
    send_first = jnp.sum(jnp.where(hot, start[None, :], 0), axis=1)
    send_last = jnp.sum(jnp.where(hot, (start + count)[None, :], 0), axis=1)

    own = half * half_slots
    keep_first = lax.dynamic_slice_in_dim(start, own, half_slots)
    keep_last = keep_first + lax.dynamic_slice_in_dim(count, own, half_slots)
    got = lax.dynamic_index_in_dim(crosses, 1 - half, 0, False)
    got = lax.dynamic_slice_in_dim(got, own, half_slots).astype(jnp.int32)
    got_first = lax.dynamic_index_in_dim(place_of, 1 - half, 0, False)
    got_first = lax.dynamic_slice_in_dim(got_first, own, half_slots)
    keep_table = jnp.concatenate([order, keep_first, keep_last, got_first, got_first + got])

    low_t = rank_cotangent(block_fill, weights, grad_out, lane_groups, rank)

    def rest(capacity, acts, low_t, up_held, order, send_first, send_last, keep_table):
        send_table = jnp.concatenate([order, send_first[:capacity], send_last[:capacity]])

        def finish(held):
            crossing = slot_sums(send_table, held, capacity)
            arrived = lax.ppermute(crossing, "dp", across)
            kept = slot_sums(keep_table, held, half_slots, arrived)
            return within(kept.reshape(half_devices, own_slots, rank, -1))

        held = [
            within(down_products(low_t, acts, half_devices, c)).reshape(half_blocks, rank, -1)
            for c in range(CHUNKS)
        ]
        up = place(finish(up_held), out_width, 0) if out_width // half_devices >= 128 else (
            finish(up_held).transpose(1, 2, 0, 3).reshape(own_slots, rank, out_width)
        )
        down = None
        for c in range(CHUNKS):
            down = place(finish(held[c]), model_width, c, down)
        return down, up

    limit = min(half_blocks, half_slots)
    capacities = sorted({-(-limit * k // 24) for k in (8, 10, 12, 16, 24)})
    index = sum((needed > c).astype(jnp.int32) for c in capacities[:-1])
    return lax.switch(
        index,
        [functools.partial(rest, c) for c in capacities],
        acts, low_t, up_held, order, send_first, send_last, keep_table,
    )


def solution(mesh):
    placed = (
        P(("groups", "dp"), None),
        P(("groups", "dp"), None),
        P(("groups", "dp"), None),
        P("dp", None, None),
        P("groups"),
        P(("groups", "dp")),
        P(),
    )
    return jax.shard_map(
        functools.partial(body, mesh.shape["dp"]),
        mesh=mesh,
        in_specs=placed,
        out_specs=(P(("groups", "dp"), None, None), P(("groups", "dp"), None, None)),
        check_vma=False,
    )
```

time: 401 us -> 222 us (0.55)
  the two profiles are of different devices: /device:TPU:15 before, /device:TPU:0 now
where the time goes in v1:
time: 222 us; the launch traced here: 224 us
  waiting for transfers between devices  130 us (59%)
  starting transfers between devices  43 us (19%)
  Pallas kernels  35 us (16%)
  local copies, waits for them, and re-layouts  6.53 us (3%)
  blocking collectives  4.89 us (2%)
  between operations  3.41 us (2%)
    ppermute x3, waiting for transfers between devices, finish(): arrived = lax.ppermute(crossing, 'dp', across)  72.5 us
    all_to_all x6, waiting for transfers between devices, within(): return lax.all_to_all(x, 'dp', 0, 0, axis_index_groups=groups, tiled=True)  33.5 us
    all_to_all x6, starting transfers between devices, within(): return lax.all_to_all(x, 'dp', 0, 0, axis_index_groups=groups, tiled=True)  26.3 us
    all_to_all x1, waiting for transfers between devices, body(): lax.all_to_all(pieces, 'dp', 0, 0, tiled=True)  14 us
    pallas_call x2, Pallas kernels, down_products(): pl.pallas_call(down_kernel, grid=(parts,), out_shape=jax.ShapeDtypeStruct...  11.5 us
    pallas_call x3, Pallas kernels, place(): pl.pallas_call(place_kernel, grid=(parts,), out_shape=jax.ShapeDtypeStruc...  11.2 us
    all_to_all x1, waiting for transfers between devices, body(): weights = lax.all_to_all(picked, 'dp', 0, 0, tiled=True)  9.55 us
    pallas_call x6, Pallas kernels, slot_sums(): pl.pallas_call(functools.partial(sum_kernel, held.shape[0], targets), out...  8.25 us
  transfers between devices with their start and end apart: 11, of which 8 were waited for; matrix products, arithmetic and copies ran while one was open for 1% of the time, Pallas kernels for 12%

profile of v1, /device:TPU:0, one launch (start us, length us, event | category | flops | bytes accessed | tf_op | source)
XLA Modules:
  0.0 224.4 jit_solution(8356664592376719385)
XLA Ops:
  3.0 7.4 %all-to-all-start.25 = ((bf16[16,4,16,256]{3,2,1,0:T(8,128)(2,1)}), bf16[16,4,16,256]{3,2,1,0:T(8,128)(2,1)S(1)}, u32[]{:S(2)}, u32[]{:S(2)}) async-start(bf16[16,4,16,256]{3,2,1,0:T(8,128)(2,1)} %bitcast.26), calls=%async_computation.25 | async-start | bytes 1048576 | tf_op jit(solution)/shard_map/all_to_all | solution.py:213
  10.9 14.0 %all-to-all-done.25 = bf16[16,4,16,256]{3,2,1,0:T(8,128)(2,1)S(1)} async-done(((bf16[16,4,16,256]{3,2,1,0:T(8,128)(2,1)}), bf16[16,4,16,256]{3,2,1,0:T(8,128)(2,1)S(1)}, u32[]{:S(2)}, u32[]{:S(2)}) %all-to-all-start.25) | async-done | bytes 524320 | tf_op jit(solution)/shard_map/all_to_all | solution.py:213
  26.5 4.1 %all-to-all-start.26 = ((bf16[16,3,16,256]{3,2,1,0:T(8,128)(2,1)}), bf16[16,3,16,256]{3,2,1,0:T(8,128)(2,1)S(1)}, u32[]{:S(2)}, u32[]{:S(2)}) async-start(bf16[16,3,16,256]{3,2,1,0:T(8,128)(2,1)} %bitcast.28), calls=%async_computation.26 | async-start | bytes 786432 | tf_op jit(solution)/shard_map/all_to_all | solution.py:215
  33.2 9.5 %all-to-all-done.26.parts_ref = bf16[16,3,16,256]{3,2,1,0:T(8,128)(2,1)S(1)} async-done(((bf16[16,3,16,256]{3,2,1,0:T(8,128)(2,1)}), bf16[16,3,16,256]{3,2,1,0:T(8,128)(2,1)S(1)}, u32[]{:S(2)}, u32[]{:S(2)}) %all-to-all-start.26) | async-done | bytes 393248 | tf_op jit(solution)/shard_map/all_to_all | solution.py:215
  42.8 3.5 %all-to-all-start.27 = ((bf16[8,3,64,128]{3,2,1,0:T(8,128)(2,1)}), bf16[8,3,64,128]{3,2,1,0:T(8,128)(2,1)S(1)}, u32[]{:S(2)}, u32[]{:S(2)}) async-start(bf16[8,3,64,128]{3,2,1,0:T(8,128)(2,1)} %shard_map.98), calls=%async_computation.27 | async-start | bytes 786432 | tf_op jit(solution)/shard_map/all_to_all | solution.py:201
  46.3 4.9 %pmax.7 = s32[]{:T(128)} all-reduce(s32[]{:T(128)} %reduce_max.9), channel_id=1, replica_groups=mesh['groups'=2,'dp'=16] {'groups'}, use_global_device_ids=true, to_apply=%region_4.5 | all-reduce | flops 1 | bytes 8 | tf_op jit(solution)/shard_map/pmax | solution.py:234
  55.4 169.0 %conditional.1 = (bf16[4,64,8192]{2,1,0:T(8,128)(2,1)}, bf16[4,64,1024]{2,1,0:T(8,128)(2,1)}) conditional(s32[]{:T(128)} %clamp.11, (bf16[3,64,128]{2,1,0:T(8,128)(2,1)S(1)}, bf16[384,8192]{1,0:T(8,128)(2,1)}, s32[24]{0:T(128)S(1)}, s32[24]{0:T(128)S(1)}, s32[24]{0:T(128)S(1)}, /*index=5*/s32[152]{0:T(256)S(1)}, ...), branch_computations={%region_12.13_spmd, %region_13.14_spmd, %region_14.15_spmd, %regio... | conditional | flops 406192256 | bytes 102761464 | solution.py:277
  58.0 8.4 %collective-permute-done.5.refs_0_ = bf16[10,64,128]{2,1,0:T(8,128)(2,1)S(1)} collective-permute-done((bf16[10,64,128]{2,1,0:T(8,128)(2,1)S(1)}, bf16[10,64,128]{2,1,0:T(8,128)(2,1)S(1)}, u32[]{:S(2)}, u32[]{:S(2)}) %collective-permute-start.5) | collective-permute-done | bytes 163872 | tf_op jit(solution)/shard_map/cond/branch_1_fun/ppermute | solution.py:258
  66.4 2.2 branch_1_fun.20
  68.6 3.5 %all-to-all-start.9 = ((bf16[8,4,64,128]{3,2,1,0:T(8,128)(2,1)}), bf16[8,4,64,128]{3,2,1,0:T(8,128)(2,1)S(1)}, u32[]{:S(2)}, u32[]{:S(2)}) async-start(bf16[8,4,64,128]{3,2,1,0:T(8,128)(2,1)} %bitcast.9), calls=%async_computation.9 | async-start | bytes 1048576 | tf_op jit(solution)/shard_map/cond/branch_1_fun/all_to_all | solution.py:201
  72.1 6.4 %branch_1_fun.14 = bf16[8,3,64,512]{3,2,1,0:T(8,128)(2,1)} custom-call(bf16[3,64,128]{2,1,0:T(8,128)(2,1)S(1)} %get-tuple-element.78.low_ref, bf16[384,8192]{1,0:T(8,128)(2,1)} %get-tuple-element.79.acts_ref), custom_call_target="tpu_custom_call" | custom-call | flops 201326592 | bytes 4718592 | tf_op jit(solution)/shard_map/cond/branch_1_fun/pallas_call | solution.py:108
  78.5 2.4 %all-to-all-done.9.got_ref = bf16[8,4,64,128]{3,2,1,0:T(8,128)(2,1)S(1)} async-done(((bf16[8,4,64,128]{3,2,1,0:T(8,128)(2,1)}), bf16[8,4,64,128]{3,2,1,0:T(8,128)(2,1)S(1)}, u32[]{:S(2)}, u32[]{:S(2)}) %all-to-all-start.9) | async-done | bytes 524320 | tf_op jit(solution)/shard_map/cond/branch_1_fun/all_to_all | solution.py:201
  80.9 3.6 %all-to-all-start.7 = ((bf16[8,3,64,512]{3,2,1,0:T(8,128)(2,1)}), bf16[8,3,64,512]{3,2,1,0:T(8,128)(2,1)S(1)}, u32[]{:S(2)}, u32[]{:S(2)}) async-start(bf16[8,3,64,512]{3,2,1,0:T(8,128)(2,1)} %branch_1_fun.14), calls=%async_computation.7 | async-start | bytes 3145728 | tf_op jit(solution)/shard_map/cond/branch_1_fun/all_to_all | solution.py:201
  84.5 5.1 %branch_1_fun.11 = bf16[8,3,64,512]{3,2,1,0:T(8,128)(2,1)S(1)} custom-call(bf16[3,64,128]{2,1,0:T(8,128)(2,1)S(1)} %get-tuple-element.78.low_ref, bf16[384,8192]{1,0:T(8,128)(2,1)} %get-tuple-element.79.acts_ref), custom_call_target="tpu_custom_call" | custom-call | flops 201326592 | bytes 4718592 | tf_op jit(solution)/shard_map/cond/branch_1_fun/pallas_call | solution.py:108
  90.8 13.7 %all-to-all-done.7 = bf16[8,3,64,512]{3,2,1,0:T(8,128)(2,1)S(1)} async-done(((bf16[8,3,64,512]{3,2,1,0:T(8,128)(2,1)}), bf16[8,3,64,512]{3,2,1,0:T(8,128)(2,1)S(1)}, u32[]{:S(2)}, u32[]{:S(2)}) %all-to-all-start.7) | async-done | bytes 1572896 | tf_op jit(solution)/shard_map/cond/branch_1_fun/all_to_all | solution.py:201
  104.5 3.6 %all-to-all-start.5 = ((bf16[8,3,64,512]{3,2,1,0:T(8,128)(2,1)}), bf16[8,3,64,512]{3,2,1,0:T(8,128)(2,1)S(1)}, u32[]{:S(2)}, u32[]{:S(2)}) async-start(bf16[8,3,64,512]{3,2,1,0:T(8,128)(2,1)} %copy-done.11), calls=%async_computation.5 | async-start | bytes 3145728 | tf_op jit(solution)/shard_map/cond/branch_1_fun/all_to_all | solution.py:201
  111.1 28.9 %collective-permute-done.4.refs_0_ = bf16[10,64,512]{2,1,0:T(8,128)(2,1)S(1)} collective-permute-done((bf16[10,64,512]{2,1,0:T(8,128)(2,1)S(1)}, bf16[10,64,512]{2,1,0:T(8,128)(2,1)S(1)}, u32[]{:S(2)}, u32[]{:S(2)}) %collective-permute-start.4) | collective-permute-done | bytes 655392 | tf_op jit(solution)/shard_map/cond/branch_1_fun/ppermute | solution.py:258
  142.9 6.4 %all-to-all-start.8 = ((bf16[8,4,64,512]{3,2,1,0:T(8,128)(2,1)}), bf16[8,4,64,512]{3,2,1,0:T(8,128)(2,1)}, u32[]{:S(2)}, u32[]{:S(2)}) async-start(bf16[8,4,64,512]{3,2,1,0:T(8,128)(2,1)} %bitcast.72), calls=%async_computation.8 | async-start | bytes 4194304 | tf_op jit(solution)/shard_map/cond/branch_1_fun/all_to_all | solution.py:201
  151.8 35.2 %collective-permute-done.3.refs_0_ = bf16[10,64,512]{2,1,0:T(8,128)(2,1)S(1)} collective-permute-done((bf16[10,64,512]{2,1,0:T(8,128)(2,1)S(1)}, bf16[10,64,512]{2,1,0:T(8,128)(2,1)S(1)}, u32[]{:S(2)}, u32[]{:S(2)}) %collective-permute-start.3) | collective-permute-done | bytes 655392 | tf_op jit(solution)/shard_map/cond/branch_1_fun/ppermute | solution.py:258
  189.9 5.8 %all-to-all-start.6 = ((bf16[8,4,64,512]{3,2,1,0:T(8,128)(2,1)}), bf16[8,4,64,512]{3,2,1,0:T(8,128)(2,1)S(1)}, u32[]{:S(2)}, u32[]{:S(2)}) async-start(bf16[8,4,64,512]{3,2,1,0:T(8,128)(2,1)} %bitcast.76), calls=%async_computation.6 | async-start | bytes 4194304 | tf_op jit(solution)/shard_map/cond/branch_1_fun/all_to_all | solution.py:201
  195.8 2.6 %branch_1_fun.21 = bf16[4,64,1024]{2,1,0:T(8,128)(2,1)} custom-call(bf16[8,4,64,128]{3,2,1,0:T(8,128)(2,1)S(1)} %copy-done.19), custom_call_target="tpu_custom_call" | custom-call | bytes 1048576 | tf_op jit(solution)/shard_map/cond/branch_1_fun/pallas_call | solution.py:174
  198.3 5.6 %branch_1_fun.17.refs_0_ = bf16[4,64,8192]{2,1,0:T(8,128)(2,1)} custom-call(bf16[8,4,64,512]{3,2,1,0:T(8,128)(2,1)} %all-to-all-done.8.got_ref), custom_call_target="tpu_custom_call" | custom-call | bytes 4194304 | tf_op jit(solution)/shard_map/cond/branch_1_fun/pallas_call | solution.py:174
  204.0 17.5 %all-to-all-done.6.got_ref = bf16[8,4,64,512]{3,2,1,0:T(8,128)(2,1)S(1)} async-done(((bf16[8,4,64,512]{3,2,1,0:T(8,128)(2,1)}), bf16[8,4,64,512]{3,2,1,0:T(8,128)(2,1)S(1)}, u32[]{:S(2)}, u32[]{:S(2)}) %all-to-all-start.6) | async-done | bytes 2097184 | tf_op jit(solution)/shard_map/cond/branch_1_fun/all_to_all | solution.py:201
  221.5 3.0 %branch_1_fun.18 = bf16[4,64,8192]{2,1,0:T(8,128)(2,1)} custom-call(bf16[8,4,64,512]{3,2,1,0:T(8,128)(2,1)S(1)} %all-to-all-done.6.got_ref, bf16[4,64,8192]{2,1,0:T(8,128)(2,1)} %branch_1_fun.17.refs_0_), custom_call_target="tpu_custom_call", output_to_operand_aliasing={{}: (1, {})} | custom-call | bytes 4194304 | tf_op jit(solution)/shard_map/cond/branch_1_fun/pallas_call | solution.py:174
  (57 shorter events, 23.8 us)
Async XLA Ops:
  0.6 9.8 %copy-start.29 = (s32[48]{0:T(128)S(1)}, s32[48]{0:T(128)}, u32[]{:S(2)}) copy-start(s32[48]{0:T(128)} %param.16) | copy-start | bytes 580
  0.6 9.8 %copy-start.28 = (s32[64]{0:T(128)S(1)}, s32[64]{0:T(128)}, u32[]{:S(2)}) copy-start(s32[64]{0:T(128)} %param.18) | copy-start | bytes 772
  2.1 29.3 %copy-start.15 = (bf16[384,1024]{1,0:T(8,128)(2,1)S(1)}, bf16[384,1024]{1,0:T(8,128)(2,1)}, u32[]{:S(2)}) copy-start(bf16[384,1024]{1,0:T(8,128)(2,1)} %grad_ref.3) | copy-start | bytes 2359300
  2.1 29.3 %copy-start.26 = (bf16[384,64]{0,1:T(8,128)(2,1)S(1)}, bf16[384,64]{0,1:T(8,128)(2,1)}, u32[]{:S(2)}) copy-start(bf16[384,64]{0,1:T(8,128)(2,1)} %param.14) | copy-start | bytes 147460
  2.1 29.2 %copy-start.27 = (s32[3]{0:T(128)S(1)}, s32[3]{0:T(128)}, u32[]{:S(2)}) copy-start(s32[3]{0:T(128)} %fill_ref.3) | copy-start | bytes 40
  3.0 21.9 %all-to-all-start.25 = ((bf16[16,4,16,256]{3,2,1,0:T(8,128)(2,1)}), bf16[16,4,16,256]{3,2,1,0:T(8,128)(2,1)S(1)}, u32[]{:S(2)}, u32[]{:S(2)}) async-start(bf16[16,4,16,256]{3,2,1,0:T(8,128)(2,1)} %bitcast.26), calls=%async_computation.25 | async-start | bytes 1048576 | tf_op jit(solution)/shard_map/all_to_all | solution.py:213
  26.5 16.3 %all-to-all-start.26 = ((bf16[16,3,16,256]{3,2,1,0:T(8,128)(2,1)}), bf16[16,3,16,256]{3,2,1,0:T(8,128)(2,1)S(1)}, u32[]{:S(2)}, u32[]{:S(2)}) async-start(bf16[16,3,16,256]{3,2,1,0:T(8,128)(2,1)} %bitcast.28), calls=%async_computation.26 | async-start | bytes 786432 | tf_op jit(solution)/shard_map/all_to_all | solution.py:215
  42.8 12.6 %all-to-all-start.27 = ((bf16[8,3,64,128]{3,2,1,0:T(8,128)(2,1)}), bf16[8,3,64,128]{3,2,1,0:T(8,128)(2,1)S(1)}, u32[]{:S(2)}, u32[]{:S(2)}) async-start(bf16[8,3,64,128]{3,2,1,0:T(8,128)(2,1)} %shard_map.98), calls=%async_computation.27 | async-start | bytes 786432 | tf_op jit(solution)/shard_map/all_to_all | solution.py:201
  56.3 10.2 %collective-permute-start.5 = (bf16[10,64,128]{2,1,0:T(8,128)(2,1)S(1)}, bf16[10,64,128]{2,1,0:T(8,128)(2,1)S(1)}, u32[]{:S(2)}, u32[]{:S(2)}) collective-permute-start(bf16[10,64,128]{2,1,0:T(8,128)(2,1)S(1)} %branch_1_fun.19), channel_id=1, source_target_pairs={{0,8},{1,9},{2,10},{3,11},{4,12},{5,13},{6,14},{7,15},{8,0},{9,1},... | collective-permute-start | bytes 491528 | tf_op jit(solution)/shard_map/cond/branch_1_fun/ppermute | solution.py:258
  68.6 12.3 %all-to-all-start.9 = ((bf16[8,4,64,128]{3,2,1,0:T(8,128)(2,1)}), bf16[8,4,64,128]{3,2,1,0:T(8,128)(2,1)S(1)}, u32[]{:S(2)}, u32[]{:S(2)}) async-start(bf16[8,4,64,128]{3,2,1,0:T(8,128)(2,1)} %bitcast.9), calls=%async_computation.9 | async-start | bytes 1048576 | tf_op jit(solution)/shard_map/cond/branch_1_fun/all_to_all | solution.py:201
  80.9 8.7 %copy-start.18 = (bf16[8,4,64,128]{3,2,1,0:T(8,128)(2,1)}, bf16[8,4,64,128]{3,2,1,0:T(8,128)(2,1)S(1)}, u32[]{:S(2)}) copy-start(bf16[8,4,64,128]{3,2,1,0:T(8,128)(2,1)S(1)} %all-to-all-done.9.got_ref) | copy-start | bytes 1572868 | tf_op jit(solution)/shard_map/cond
  80.9 23.6 %all-to-all-start.7 = ((bf16[8,3,64,512]{3,2,1,0:T(8,128)(2,1)}), bf16[8,3,64,512]{3,2,1,0:T(8,128)(2,1)S(1)}, u32[]{:S(2)}, u32[]{:S(2)}) async-start(bf16[8,3,64,512]{3,2,1,0:T(8,128)(2,1)} %branch_1_fun.14), calls=%async_computation.7 | async-start | bytes 3145728 | tf_op jit(solution)/shard_map/cond/branch_1_fun/all_to_all | solution.py:201
  89.6 1.2 copy-start.11
  104.5 38.5 %all-to-all-start.5 = ((bf16[8,3,64,512]{3,2,1,0:T(8,128)(2,1)}), bf16[8,3,64,512]{3,2,1,0:T(8,128)(2,1)S(1)}, u32[]{:S(2)}, u32[]{:S(2)}) async-start(bf16[8,3,64,512]{3,2,1,0:T(8,128)(2,1)} %copy-done.11), calls=%async_computation.5 | async-start | bytes 3145728 | tf_op jit(solution)/shard_map/cond/branch_1_fun/all_to_all | solution.py:201
  109.1 30.9 %collective-permute-start.4 = (bf16[10,64,512]{2,1,0:T(8,128)(2,1)S(1)}, bf16[10,64,512]{2,1,0:T(8,128)(2,1)S(1)}, u32[]{:S(2)}, u32[]{:S(2)}) collective-permute-start(bf16[10,64,512]{2,1,0:T(8,128)(2,1)S(1)} %branch_1_fun.15), channel_id=1, source_target_pairs={{0,8},{1,9},{2,10},{3,11},{4,12},{5,13},{6,14},{7,15},{8,0},{9,1},... | collective-permute-start | bytes 1966088 | tf_op jit(solution)/shard_map/cond/branch_1_fun/ppermute | solution.py:258
  141.6 1.3 copy-start.1
  142.9 47.0 %all-to-all-start.8 = ((bf16[8,4,64,512]{3,2,1,0:T(8,128)(2,1)}), bf16[8,4,64,512]{3,2,1,0:T(8,128)(2,1)}, u32[]{:S(2)}, u32[]{:S(2)}) async-start(bf16[8,4,64,512]{3,2,1,0:T(8,128)(2,1)} %bitcast.72), calls=%async_computation.8 | async-start | bytes 4194304 | tf_op jit(solution)/shard_map/cond/branch_1_fun/all_to_all | solution.py:201
  150.4 36.6 %collective-permute-start.3 = (bf16[10,64,512]{2,1,0:T(8,128)(2,1)S(1)}, bf16[10,64,512]{2,1,0:T(8,128)(2,1)S(1)}, u32[]{:S(2)}, u32[]{:S(2)}) collective-permute-start(bf16[10,64,512]{2,1,0:T(8,128)(2,1)S(1)} %branch_1_fun.12), channel_id=1, source_target_pairs={{0,8},{1,9},{2,10},{3,11},{4,12},{5,13},{6,14},{7,15},{8,0},{9,1},... | collective-permute-start | bytes 1966088 | tf_op jit(solution)/shard_map/cond/branch_1_fun/ppermute | solution.py:258
  188.6 1.3 copy-start.5
  189.9 5.8 %copy-start.19 = (bf16[8,4,64,128]{3,2,1,0:T(8,128)(2,1)S(1)}, bf16[8,4,64,128]{3,2,1,0:T(8,128)(2,1)}, u32[]{:S(2)}) copy-start(bf16[8,4,64,128]{3,2,1,0:T(8,128)(2,1)} %copy-done.18) | copy-start | bytes 1572868 | tf_op jit(solution)/shard_map/cond
  189.9 31.5 %all-to-all-start.6 = ((bf16[8,4,64,512]{3,2,1,0:T(8,128)(2,1)}), bf16[8,4,64,512]{3,2,1,0:T(8,128)(2,1)S(1)}, u32[]{:S(2)}, u32[]{:S(2)}) async-start(bf16[8,4,64,512]{3,2,1,0:T(8,128)(2,1)} %bitcast.76), calls=%async_computation.6 | async-start | bytes 4194304 | tf_op jit(solution)/shard_map/cond/branch_1_fun/all_to_all | solution.py:201

commit v2 on v1

--- a/solution.py
+++ b/solution.py
@@ -56,14 +56,16 @@
             preferred_element_type=F32,
         )
         live = lax.broadcasted_iota(jnp.int32, low.shape, 1) < fill_ref[b]
-        out_ref[b] = jnp.where(live, low, 0.0).astype(BF16)
-
-
-def rank_cotangent(fill, parts, grad, lane_groups, rank):
+        low = jnp.where(live, low, 0.0).astype(BF16)
+        for d in range(out_ref.shape[0]):
+            out_ref[d, b] = low
+
+
+def rank_cotangent(fill, parts, grad, lane_groups, rank, copies):
     blocks = fill.shape[0]
     return pl.pallas_call(
         functools.partial(low_kernel, lane_groups),
-        out_shape=jax.ShapeDtypeStruct((blocks, rank, BLOCK), BF16),
+        out_shape=jax.ShapeDtypeStruct((copies, blocks, rank, BLOCK), BF16),
         in_specs=[pl.BlockSpec(memory_space=pltpu.SMEM), spec(), spec()],
         out_specs=spec(),
         scratch_shapes=[pltpu.VMEM((blocks, rank, grad.shape[1]), BF16)],
@@ -95,22 +97,41 @@
     )(fill, low_t, grad)
 
 
+def split_kernel(acts_ref, out_ref):
+    out_ref[0] = acts_ref[...]
+
+
+def split(acts, parts, chunk):
+    rows, width = acts.shape[0], acts.shape[1] // (parts * CHUNKS)
+    return pl.pallas_call(
+        split_kernel,
+        grid=(parts,),
+        out_shape=jax.ShapeDtypeStruct((parts, rows, width), BF16),
+        in_specs=[pl.BlockSpec((rows, width), lambda p: (0, chunk * parts + p))],
+        out_specs=pl.BlockSpec((1, rows, width), lambda p: (p, 0, 0)),
+        compiler_params=params(),
+        cost_estimate=pl.CostEstimate(
+            flops=0, bytes_accessed=4 * parts * rows * width, transcendentals=0
+        ),
+    )(acts)
+
+
 def down_kernel(low_ref, acts_ref, out_ref):
-    for b in range(low_ref.shape[0]):
+    for b in range(low_ref.shape[1]):
         out_ref[0, b] = jnp.dot(
-            low_ref[b], acts_ref[b * BLOCK : (b + 1) * BLOCK, :], preferred_element_type=F32
+            low_ref[0, b], acts_ref[b * BLOCK : (b + 1) * BLOCK, :], preferred_element_type=F32
         ).astype(BF16)
 
 
 def down_products(low_t, acts, parts, chunk):
-    blocks, rank, _ = low_t.shape
+    _, blocks, rank, _ = low_t.shape
     rows, width = acts.shape[0], acts.shape[1] // (parts * CHUNKS)
     return pl.pallas_call(
         down_kernel,
         grid=(parts,),
         out_shape=jax.ShapeDtypeStruct((parts, blocks, rank, width), BF16),
         in_specs=[
-            pl.BlockSpec(low_t.shape, lambda p: (0, 0, 0)),
+            pl.BlockSpec((1,) + low_t.shape[1:], lambda p: (0, 0, 0, 0)),
             pl.BlockSpec((rows, width), lambda p: (0, chunk * parts + p)),
         ],
         out_specs=pl.BlockSpec((1, blocks, rank, width), lambda p: (p, 0, 0, 0)),
@@ -123,44 +144,64 @@
     )(low_t, acts)
 
 
-def sum_kernel(blocks, targets, table_ref, held_ref, *refs):
-    extra_ref, out_ref = refs if len(refs) == 2 else (None, refs[0])
+def sum_kernel(blocks, targets, taken, table_ref, *refs):
+    held_ref, extra_ref, out_ref = refs[-3], refs[-2], refs[-1]
+    rank, whole = out_ref.shape[1:]
+    width = held_ref.shape[2]
     first, last = blocks, blocks + targets
+    place = last + targets
 
     def step(t, carry):
+        begin, end = table_ref[first + t], table_ref[last + t]
+
         def add(j, total):
             return total + held_ref[table_ref[j]].astype(F32)
 
-        total = lax.fori_loop(
-            table_ref[first + t], table_ref[last + t], add, jnp.zeros(out_ref.shape[1:], F32)
-        )
-        if extra_ref is not None:
-            place = last + targets
-
+        def extras(low, high, total):
             def add_extra(j, total):
-                return total + extra_ref[j].astype(F32)
-
-            total = lax.fori_loop(
+                return total + extra_ref[j, :, low:high].astype(F32)
+
+            if extra_ref is None:
+                return total
+            return lax.fori_loop(
                 table_ref[place + t], table_ref[place + targets + t], add_extra, total
             )
-        out_ref[t] = total.astype(BF16)
+
+        total = lax.fori_loop(begin, end, add, jnp.zeros((rank, width), F32))
+        out_ref[t, :, whole - width :] = extras(whole - width, whole, total).astype(BF16)
+        if taken:
+            low_ref, rows_ref = refs[0], refs[1]
+
+            def multiply(j, total):
+                b = table_ref[j]
+                return total + jnp.dot(low_ref[b], rows_ref[b], preferred_element_type=F32)
+
+            total = lax.fori_loop(begin, end, multiply, jnp.zeros((rank, whole - width), F32))
+            out_ref[t, :, : whole - width] = extras(0, whole - width, total).astype(BF16)
         return carry
 
     lax.fori_loop(0, targets, step, 0)
 
 
-def slot_sums(table, held, targets, extra=None):
-    operands = (held,) if extra is None else (held, extra)
-    size = held.shape[1] * held.shape[2]
-    moved = 2 * size * (targets + sum(x.shape[0] for x in operands))
-    return pl.pallas_call(
-        functools.partial(sum_kernel, held.shape[0], targets),
-        out_shape=jax.ShapeDtypeStruct((targets,) + held.shape[1:], BF16),
+def sum_only_kernel(blocks, targets, taken, table_ref, *refs):
+    sum_kernel(blocks, targets, taken, table_ref, *refs[:-1], None, refs[-1])
+
+
+def slot_sums(table, held, targets, extra=None, taken=()):
+    blocks, rank, width = held.shape
+    whole = width + (taken[1].shape[2] if taken else 0)
+    operands = tuple(taken) + (held,) + (() if extra is None else (extra,))
+    moved = 2 * targets * rank * whole + 2 * sum(x.size for x in operands)
+    return pl.pallas_call(
+        functools.partial(
+            sum_only_kernel if extra is None else sum_kernel, blocks, targets, bool(taken)
+        ),
+        out_shape=jax.ShapeDtypeStruct((targets, rank, whole), BF16),
         in_specs=[pl.BlockSpec(memory_space=pltpu.SMEM)] + [spec()] * len(operands),
         out_specs=spec(),
         compiler_params=params(),
         cost_estimate=pl.CostEstimate(
-            flops=size * held.shape[0], bytes_accessed=moved, transcendentals=0
+            flops=2 * BLOCK * rank * whole * blocks, bytes_accessed=moved, transcendentals=0
         ),
     )(table, *operands)
 
@@ -169,8 +210,8 @@
     refs[-1][...] = got_ref[0]
 
 
-def place(got, columns, chunk, into=None):
-    parts, slots, rank, width = got.shape
+def place(got, width, columns, chunk, into=None):
+    parts, slots, rank, _ = got.shape
     return pl.pallas_call(
         place_kernel,
         grid=(parts,),
@@ -186,7 +227,7 @@
     )(*((got,) if into is None else (got, into)))
 
 
-def body(devices, acts, grad_out, low_acts, up_weight, block_adapter, block_fill, owner_slot):
+def body(copies, devices, acts, grad_out, low_acts, up_weight, block_adapter, block_fill, owner_slot):
     own_blocks = block_fill.shape[0]
     blocks, adapters = block_adapter.shape[0], owner_slot.shape[0]
     own_slots, rank, out_width = up_weight.shape
@@ -231,7 +272,12 @@
     crosses = has & ((ids[None, :] // half_slots) != jnp.arange(2, dtype=jnp.int32)[:, None])
     earlier = (ids[None, :] < ids[:, None])[None, :, :]
     place_of = jnp.sum((crosses[:, None, :] & earlier).astype(jnp.int32), axis=2)
-    needed = lax.pmax(jnp.max(jnp.sum(crosses.astype(jnp.int32), axis=1)), "groups")
+    mine_needed = jnp.max(jnp.sum(crosses.astype(jnp.int32), axis=1)).reshape(1, 1)
+    needed = mine_needed
+    for k in range(1, copies):
+        shift = [(i, (i + k) % copies) for i in range(copies)]
+        needed = jnp.maximum(needed, lax.ppermute(mine_needed, "groups", shift))
+    needed = needed[0, 0]
 
     my_cross = lax.dynamic_index_in_dim(crosses, half, 0, False)
     my_place = lax.dynamic_index_in_dim(place_of, half, 0, False)
@@ -248,27 +294,26 @@
     got_first = lax.dynamic_slice_in_dim(got_first, own, half_slots)
     keep_table = jnp.concatenate([order, keep_first, keep_last, got_first, got_first + got])
 
-    low_t = rank_cotangent(block_fill, weights, grad_out, lane_groups, rank)
-
-    def rest(capacity, acts, low_t, up_held, order, send_first, send_last, keep_table):
+    low_t = rank_cotangent(block_fill, weights, grad_out, lane_groups, rank, half_devices)
+    all_low = within(low_t).reshape(half_blocks, rank, BLOCK)
+    rows_held = within(split(acts, half_devices, 0)).reshape(half_blocks, BLOCK, -1)
+    held = within(down_products(low_t, acts, half_devices, 1)).reshape(half_blocks, rank, -1)
+
+    def rest(capacity, all_low, rows_held, held, up_held, order, send_first, send_last, keep_table):
         send_table = jnp.concatenate([order, send_first[:capacity], send_last[:capacity]])
 
-        def finish(held):
-            crossing = slot_sums(send_table, held, capacity)
+        def finish(held, taken=()):
+            crossing = slot_sums(send_table, held, capacity, None, taken)
             arrived = lax.ppermute(crossing, "dp", across)
-            kept = slot_sums(keep_table, held, half_slots, arrived)
+            kept = slot_sums(keep_table, held, half_slots, arrived, taken)
             return within(kept.reshape(half_devices, own_slots, rank, -1))
 
-        held = [
-            within(down_products(low_t, acts, half_devices, c)).reshape(half_blocks, rank, -1)
-            for c in range(CHUNKS)
-        ]
-        up = place(finish(up_held), out_width, 0) if out_width // half_devices >= 128 else (
-            finish(up_held).transpose(1, 2, 0, 3).reshape(own_slots, rank, out_width)
-        )
-        down = None
-        for c in range(CHUNKS):
-            down = place(finish(held[c]), model_width, c, down)
+        first = finish(up_held, (all_low, rows_held))
+        second = finish(held)
+        width = rows_held.shape[2]
+        up = first[:, :, :, width:].transpose(1, 2, 0, 3).reshape(own_slots, rank, out_width)
+        down = place(first, width, model_width, 0)
+        down = place(second, width, model_width, 1, down)
         return down, up
 
     limit = min(half_blocks, half_slots)
@@ -277,7 +322,7 @@
     return lax.switch(
         index,
         [functools.partial(rest, c) for c in capacities],
-        acts, low_t, up_held, order, send_first, send_last, keep_table,
+        all_low, rows_held, held, up_held, order, send_first, send_last, keep_table,
     )
 
 
@@ -292,7 +337,7 @@
         P(),
     )
     return jax.shard_map(
-        functools.partial(body, mesh.shape["dp"]),
+        functools.partial(body, mesh.shape["groups"], mesh.shape["dp"]),
         mesh=mesh,
         in_specs=placed,
         out_specs=(P(("groups", "dp"), None, None), P(("groups", "dp"), None, None)),

time: 222 us -> 267 us (1.20); the launches traced: 224 us -> 266 us
  waiting for transfers between devices: 130 us -> 176 us
  blocking collectives: 4.89 us -> 0 us
  Pallas kernels: 35 us -> 39 us
    all_to_all x6, waiting for transfers between devices: 33.5 us -> 73.6 us  [within(): return lax.all_to_all(x, 'dp', 0, 0, axis_index_groups=groups, tiled=True)]
    pallas_call x6 -> x5, Pallas kernels: 8.25 us -> 19.1 us  [the longest x4 12.9 us: slot_sums(): pl.pallas_call(functools.partial(sum_only_kernel if extra is None else su...]
    pallas_call x2 -> x1, Pallas kernels: 11.5 us -> 6.4 us  [down_products(): pl.pallas_call(down_kernel, grid=(parts,), out_shape=jax.ShapeDtypeStruct...]
    pmax x1 -> x0, blocking collectives: 4.89 us -> none  [body(): lax.pmax(jnp.max(jnp.sum(crosses.astype(jnp.int32), axis=1)), 'groups')]
    ppermute x3 -> x2, waiting for transfers between devices: 72.5 us -> 76.4 us  [finish(): arrived = lax.ppermute(crossing, 'dp', across)]
    pallas_call x3 -> x2, Pallas kernels: 11.2 us -> 8.71 us  [place(): pl.pallas_call(place_kernel, grid=(parts,), out_shape=jax.ShapeDtypeStruc...]
  transfers between devices with their start and end apart: 11 -> 11, of which waited for: 8 -> 10; matrix products, arithmetic and copies ran while one was open for 1% -> 1% of each run, Pallas kernels for 12% -> 8%
where the time goes in v2:
time: 267 us; the launch traced here: 266 us
  waiting for transfers between devices  176 us (66%)
  starting transfers between devices  40.6 us (15%)
  Pallas kernels  39 us (15%)
  local copies, waits for them, and re-layouts  6.41 us (2%)
    ppermute x2, waiting for transfers between devices, finish(): arrived = lax.ppermute(crossing, 'dp', across)  76.4 us
    all_to_all x6, waiting for transfers between devices, within(): return lax.all_to_all(x, 'dp', 0, 0, axis_index_groups=groups, tiled=True)  73.6 us
    all_to_all x6, starting transfers between devices, within(): return lax.all_to_all(x, 'dp', 0, 0, axis_index_groups=groups, tiled=True)  24.4 us
    all_to_all x1, waiting for transfers between devices, body(): lax.all_to_all(pieces, 'dp', 0, 0, tiled=True)  14.3 us
    pallas_call x4, Pallas kernels, slot_sums(): pl.pallas_call(functools.partial(sum_only_kernel if extra is None else su...  12.9 us
    all_to_all x1, waiting for transfers between devices, body(): weights = lax.all_to_all(picked, 'dp', 0, 0, tiled=True)  10.6 us
    pallas_call x2, Pallas kernels, place(): pl.pallas_call(place_kernel, grid=(parts,), out_shape=jax.ShapeDtypeStruc...  8.71 us
    all_to_all x1, starting transfers between devices, body(): lax.all_to_all(pieces, 'dp', 0, 0, tiled=True)  7.39 us
  transfers between devices with their start and end apart: 11, of which 10 were waited for; matrix products, arithmetic and copies ran while one was open for 1% of the time, Pallas kernels for 8%

profile of v2, /device:TPU:0, one launch (start us, length us, event | category | flops | bytes accessed | tf_op | source)
XLA Modules:
  0.0 266.0 jit_solution(10502921561994535920)
XLA Ops:
  3.1 7.4 %all-to-all-start.10 = ((bf16[16,4,16,256]{3,2,1,0:T(8,128)(2,1)}), bf16[16,4,16,256]{3,2,1,0:T(8,128)(2,1)S(1)}, u32[]{:S(2)}, u32[]{:S(2)}) async-start(bf16[16,4,16,256]{3,2,1,0:T(8,128)(2,1)} %bitcast.20), calls=%async_computation.10 | async-start | bytes 1048576 | tf_op jit(solution)/shard_map/all_to_all | solution.py:254
  10.7 14.3 %all-to-all-done.10 = bf16[16,4,16,256]{3,2,1,0:T(8,128)(2,1)S(1)} async-done(((bf16[16,4,16,256]{3,2,1,0:T(8,128)(2,1)}), bf16[16,4,16,256]{3,2,1,0:T(8,128)(2,1)S(1)}, u32[]{:S(2)}, u32[]{:S(2)}) %all-to-all-start.10) | async-done | bytes 524320 | tf_op jit(solution)/shard_map/all_to_all | solution.py:254
  26.5 4.1 %all-to-all-start.11 = ((bf16[16,3,16,256]{3,2,1,0:T(8,128)(2,1)}), bf16[16,3,16,256]{3,2,1,0:T(8,128)(2,1)S(1)}, u32[]{:S(2)}, u32[]{:S(2)}) async-start(bf16[16,3,16,256]{3,2,1,0:T(8,128)(2,1)} %bitcast.22), calls=%async_computation.11 | async-start | bytes 786432 | tf_op jit(solution)/shard_map/all_to_all | solution.py:256
  32.2 10.6 %all-to-all-done.11.parts_ref = bf16[16,3,16,256]{3,2,1,0:T(8,128)(2,1)S(1)} async-done(((bf16[16,3,16,256]{3,2,1,0:T(8,128)(2,1)}), bf16[16,3,16,256]{3,2,1,0:T(8,128)(2,1)S(1)}, u32[]{:S(2)}, u32[]{:S(2)}) %all-to-all-start.11) | async-done | bytes 393248 | tf_op jit(solution)/shard_map/all_to_all | solution.py:256
  42.8 3.5 %all-to-all-start.15 = ((bf16[8,3,64,128]{3,2,1,0:T(8,128)(2,1)}), bf16[8,3,64,128]{3,2,1,0:T(8,128)(2,1)S(1)}, u32[]{:S(2)}, u32[]{:S(2)}) async-start(bf16[8,3,64,128]{3,2,1,0:T(8,128)(2,1)} %shard_map.100), calls=%async_computation.15 | async-start | bytes 786432 | tf_op jit(solution)/shard_map/all_to_all | solution.py:242
  48.0 5.7 %all-to-all-done.15 = bf16[8,3,64,128]{3,2,1,0:T(8,128)(2,1)S(1)} async-done(((bf16[8,3,64,128]{3,2,1,0:T(8,128)(2,1)}), bf16[8,3,64,128]{3,2,1,0:T(8,128)(2,1)S(1)}, u32[]{:S(2)}, u32[]{:S(2)}) %all-to-all-start.15) | async-done | bytes 393248 | tf_op jit(solution)/shard_map/all_to_all | solution.py:242
  53.7 3.5 %all-to-all-start.13 = ((bf16[8,3,64,128]{3,2,1,0:T(8,128)(2,1)}), bf16[8,3,64,128]{3,2,1,0:T(8,128)(2,1)S(1)}, u32[]{:S(2)}, u32[]{:S(2)}) async-start(bf16[8,3,64,128]{3,2,1,0:T(8,128)(2,1)} %shard_map.97.low_ref), calls=%async_computation.13 | async-start | bytes 786432 | tf_op jit(solution)/shard_map/all_to_all | solution.py:242
  57.2 6.4 %shard_map.98 = bf16[8,3,64,512]{3,2,1,0:T(8,128)(2,1)} custom-call(bf16[8,3,64,128]{3,2,1,0:T(8,128)(2,1)} %shard_map.97.low_ref, bf16[384,8192]{1,0:T(8,128)(2,1)} %acts_ref.3), custom_call_target="tpu_custom_call" | custom-call | flops 201326592 | bytes 4718592 | tf_op jit(solution)/shard_map/pallas_call | solution.py:129
  64.6 4.3 %all-to-all-start.12 = ((bf16[8,3,64,512]{3,2,1,0:T(8,128)(2,1)}), bf16[8,3,64,512]{3,2,1,0:T(8,128)(2,1)}, u32[]{:S(2)}, u32[]{:S(2)}) async-start(bf16[8,3,64,512]{3,2,1,0:T(8,128)(2,1)} %shard_map.98), calls=%async_computation.12 | async-start | bytes 3145728 | tf_op jit(solution)/shard_map/all_to_all | solution.py:242
  68.9 6.1 %shard_map.99 = bf16[8,384,512]{2,1,0:T(8,128)(2,1)} custom-call(bf16[384,8192]{1,0:T(8,128)(2,1)} %acts_ref.3), custom_call_target="tpu_custom_call" | custom-call | bytes 6291456 | tf_op jit(solution)/shard_map/pallas_call | solution.py:106
  75.0 14.0 %all-to-all-done.12 = bf16[8,3,64,512]{3,2,1,0:T(8,128)(2,1)} async-done(((bf16[8,3,64,512]{3,2,1,0:T(8,128)(2,1)}), bf16[8,3,64,512]{3,2,1,0:T(8,128)(2,1)}, u32[]{:S(2)}, u32[]{:S(2)}) %all-to-all-start.12) | async-done | bytes 1572896 | tf_op jit(solution)/shard_map/all_to_all | solution.py:242
  88.9 4.5 %all-to-all-start.14 = ((bf16[8,384,512]{2,1,0:T(8,128)(2,1)}), bf16[8,384,512]{2,1,0:T(8,128)(2,1)}, u32[]{:S(2)}, u32[]{:S(2)}) async-start(bf16[8,384,512]{2,1,0:T(8,128)(2,1)} %shard_map.99), calls=%async_computation.14 | async-start | bytes 6291456 | tf_op jit(solution)/shard_map/all_to_all | solution.py:242
  99.3 31.1 %all-to-all-done.14 = bf16[8,384,512]{2,1,0:T(8,128)(2,1)} async-done(((bf16[8,384,512]{2,1,0:T(8,128)(2,1)}), bf16[8,384,512]{2,1,0:T(8,128)(2,1)}, u32[]{:S(2)}, u32[]{:S(2)}) %all-to-all-start.14) | async-done | bytes 3145760 | tf_op jit(solution)/shard_map/all_to_all | solution.py:242
  130.3 135.7 %conditional.1 = (bf16[4,64,8192]{2,1,0:T(8,128)(2,1)}, bf16[4,64,1024]{2,1,0:T(8,128)(2,1)}) conditional(s32[]{:T(128)} %bitcast.16, (s32[24]{0:T(128)S(1)}, s32[24]{0:T(128)S(1)}, s32[24]{0:T(128)S(1)}, bf16[24,64,512]{2,1,0:T(8,128)(2,1)}, s32[152]{0:T(256)S(1)}, /*index=5*/bf16[24,64,128]{2,1,0:T(8,128)(2,1)S(1)}, ...), branch_computations={%region_11.12_spmd, %region_12.13_spmd, %region_13.14_spmd, %regio... | conditional | flops 905969792 | bytes 85721904 | solution.py:322
  130.4 3.6 %branch_1_fun.8 = bf16[10,64,640]{2,1,0:T(8,128)(2,1)S(1)} custom-call(s32[44]{0:T(128)S(1)} %pad_add_fusion.1.table_ref, bf16[24,64,128]{2,1,0:T(8,128)(2,1)S(1)} %get-tuple-element.93.refs_0_, bf16[24,128,512]{2,1,0:T(8,128)(2,1)} %get-tuple-element.94.refs_1_, bf16[24,64,128]{2,1,0:T(8,128)(2,1)S(1)} %get-tuple-element.95.refs_2_), custom_call_target="tpu_custom_call" | custom-call | flops 251658240 | bytes 4751360 | tf_op jit(solution)/shard_map/cond/branch_1_fun/pallas_call | solution.py:195
  134.0 2.2 collective-permute-start.3
  136.2 36.1 %collective-permute-done.3.refs_3_ = bf16[10,64,640]{2,1,0:T(8,128)(2,1)S(1)} collective-permute-done((bf16[10,64,640]{2,1,0:T(8,128)(2,1)S(1)}, bf16[10,64,640]{2,1,0:T(8,128)(2,1)S(1)}, u32[]{:S(2)}, u32[]{:S(2)}) %collective-permute-start.3) | collective-permute-done | bytes 819232 | tf_op jit(solution)/shard_map/cond/branch_1_fun/ppermute | solution.py:307
  172.3 5.7 %branch_1_fun.9 = bf16[32,64,640]{2,1,0:T(8,128)(2,1)S(1)} custom-call(s32[152]{0:T(256)S(1)} %get-tuple-element.88.table_ref, bf16[24,64,128]{2,1,0:T(8,128)(2,1)S(1)} %get-tuple-element.93.refs_0_, bf16[24,128,512]{2,1,0:T(8,128)(2,1)} %get-tuple-element.94.refs_1_, bf16[24,64,128]{2,1,0:T(8,128)(2,1)S(1)} %get-tuple-element.95.refs_2_, ...), custom_call_target="tpu_custom_call" | custom-call | flops 251658240 | bytes 7372800 | tf_op jit(solution)/shard_map/cond/branch_1_fun/pallas_call | solution.py:195
  179.5 3.6 %all-to-all-start.3 = ((bf16[8,4,64,640]{3,2,1,0:T(8,128)(2,1)}), bf16[8,4,64,640]{3,2,1,0:T(8,128)(2,1)S(1)}, u32[]{:S(2)}, u32[]{:S(2)}) async-start(bf16[8,4,64,640]{3,2,1,0:T(8,128)(2,1)} %bitcast.71), calls=%async_computation.3 | async-start | bytes 5242880 | tf_op jit(solution)/shard_map/cond/branch_1_fun/all_to_all | solution.py:242
  186.0 40.3 %collective-permute-done.2.refs_1_ = bf16[10,64,512]{2,1,0:T(8,128)(2,1)S(1)} collective-permute-done((bf16[10,64,512]{2,1,0:T(8,128)(2,1)S(1)}, bf16[10,64,512]{2,1,0:T(8,128)(2,1)S(1)}, u32[]{:S(2)}, u32[]{:S(2)}) %collective-permute-start.2) | collective-permute-done | bytes 655392 | tf_op jit(solution)/shard_map/cond/branch_1_fun/ppermute | solution.py:307
  229.4 5.2 %all-to-all-start.2 = ((bf16[8,4,64,512]{3,2,1,0:T(8,128)(2,1)}), bf16[8,4,64,512]{3,2,1,0:T(8,128)(2,1)}, u32[]{:S(2)}, u32[]{:S(2)}) async-start(bf16[8,4,64,512]{3,2,1,0:T(8,128)(2,1)} %bitcast.77), calls=%async_computation.2 | async-start | bytes 4194304 | tf_op jit(solution)/shard_map/cond/branch_1_fun/all_to_all | solution.py:242
  234.6 3.1 %branch_1_fun.10.refs_0_ = bf16[4,64,8192]{2,1,0:T(8,128)(2,1)} custom-call(bf16[8,4,64,640]{3,2,1,0:T(8,128)(2,1)S(1)} %all-to-all-done.3.got_ref), custom_call_target="tpu_custom_call" | custom-call | bytes 4194304 | tf_op jit(solution)/shard_map/cond/branch_1_fun/pallas_call | solution.py:215
  238.5 21.9 %all-to-all-done.2.got_ref = bf16[8,4,64,512]{3,2,1,0:T(8,128)(2,1)} async-done(((bf16[8,4,64,512]{3,2,1,0:T(8,128)(2,1)}), bf16[8,4,64,512]{3,2,1,0:T(8,128)(2,1)}, u32[]{:S(2)}, u32[]{:S(2)}) %all-to-all-start.2) | async-done | bytes 2097184 | tf_op jit(solution)/shard_map/cond/branch_1_fun/all_to_all | solution.py:242
  260.4 5.6 %branch_1_fun.11 = bf16[4,64,8192]{2,1,0:T(8,128)(2,1)} custom-call(bf16[8,4,64,512]{3,2,1,0:T(8,128)(2,1)} %all-to-all-done.2.got_ref, bf16[4,64,8192]{2,1,0:T(8,128)(2,1)} %branch_1_fun.10.refs_0_), custom_call_target="tpu_custom_call", output_to_operand_aliasing={{}: (1, {})} | custom-call | bytes 4194304 | tf_op jit(solution)/shard_map/cond/branch_1_fun/pallas_call | solution.py:215
  (50 shorter events, 21.3 us)
Async XLA Ops:
  0.6 9.8 %copy-start.18 = (s32[64]{0:T(128)S(1)}, s32[64]{0:T(128)}, u32[]{:S(2)}) copy-start(s32[64]{0:T(128)} %param.18) | copy-start | bytes 772
  0.6 9.8 %copy-start.19 = (s32[48]{0:T(128)S(1)}, s32[48]{0:T(128)}, u32[]{:S(2)}) copy-start(s32[48]{0:T(128)} %param.16) | copy-start | bytes 580
  0.7 30.0 %copy-start.12 = (s32[3]{0:T(128)S(1)}, s32[3]{0:T(128)}, u32[]{:S(2)}) copy-start(s32[3]{0:T(128)} %fill_ref.3) | copy-start | bytes 40
  0.7 30.0 %copy-start.10 = (bf16[384,1024]{1,0:T(8,128)(2,1)S(1)}, bf16[384,1024]{1,0:T(8,128)(2,1)}, u32[]{:S(2)}) copy-start(bf16[384,1024]{1,0:T(8,128)(2,1)} %grad_ref.3) | copy-start | bytes 2359300
  0.7 30.0 %copy-start.11 = (bf16[384,64]{0,1:T(8,128)(2,1)S(1)}, bf16[384,64]{0,1:T(8,128)(2,1)}, u32[]{:S(2)}) copy-start(bf16[384,64]{0,1:T(8,128)(2,1)} %param.14) | copy-start | bytes 147460
  3.1 21.9 %all-to-all-start.10 = ((bf16[16,4,16,256]{3,2,1,0:T(8,128)(2,1)}), bf16[16,4,16,256]{3,2,1,0:T(8,128)(2,1)S(1)}, u32[]{:S(2)}, u32[]{:S(2)}) async-start(bf16[16,4,16,256]{3,2,1,0:T(8,128)(2,1)} %bitcast.20), calls=%async_computation.10 | async-start | bytes 1048576 | tf_op jit(solution)/shard_map/all_to_all | solution.py:254
  26.5 16.3 %all-to-all-start.11 = ((bf16[16,3,16,256]{3,2,1,0:T(8,128)(2,1)}), bf16[16,3,16,256]{3,2,1,0:T(8,128)(2,1)S(1)}, u32[]{:S(2)}, u32[]{:S(2)}) async-start(bf16[16,3,16,256]{3,2,1,0:T(8,128)(2,1)} %bitcast.22), calls=%async_computation.11 | async-start | bytes 786432 | tf_op jit(solution)/shard_map/all_to_all | solution.py:256
  42.8 10.9 %all-to-all-start.15 = ((bf16[8,3,64,128]{3,2,1,0:T(8,128)(2,1)}), bf16[8,3,64,128]{3,2,1,0:T(8,128)(2,1)S(1)}, u32[]{:S(2)}, u32[]{:S(2)}) async-start(bf16[8,3,64,128]{3,2,1,0:T(8,128)(2,1)} %shard_map.100), calls=%async_computation.15 | async-start | bytes 786432 | tf_op jit(solution)/shard_map/all_to_all | solution.py:242
  53.7 10.9 %all-to-all-start.13 = ((bf16[8,3,64,128]{3,2,1,0:T(8,128)(2,1)}), bf16[8,3,64,128]{3,2,1,0:T(8,128)(2,1)S(1)}, u32[]{:S(2)}, u32[]{:S(2)}) async-start(bf16[8,3,64,128]{3,2,1,0:T(8,128)(2,1)} %shard_map.97.low_ref), calls=%async_computation.13 | async-start | bytes 786432 | tf_op jit(solution)/shard_map/all_to_all | solution.py:242
  64.6 24.4 %all-to-all-start.12 = ((bf16[8,3,64,512]{3,2,1,0:T(8,128)(2,1)}), bf16[8,3,64,512]{3,2,1,0:T(8,128)(2,1)}, u32[]{:S(2)}, u32[]{:S(2)}) async-start(bf16[8,3,64,512]{3,2,1,0:T(8,128)(2,1)} %shard_map.98), calls=%async_computation.12 | async-start | bytes 3145728 | tf_op jit(solution)/shard_map/all_to_all | solution.py:242
  88.9 41.4 %all-to-all-start.14 = ((bf16[8,384,512]{2,1,0:T(8,128)(2,1)}), bf16[8,384,512]{2,1,0:T(8,128)(2,1)}, u32[]{:S(2)}, u32[]{:S(2)}) async-start(bf16[8,384,512]{2,1,0:T(8,128)(2,1)} %shard_map.99), calls=%async_computation.14 | async-start | bytes 6291456 | tf_op jit(solution)/shard_map/all_to_all | solution.py:242
  94.3 3.6 %collective-permute-start.10 = (s32[1,1]{1,0:T(1,128)}, s32[1,1]{1,0:T(1,128)}, u32[]{:S(2)}, u32[]{:S(2)}) collective-permute-start(s32[1,1]{1,0:T(1,128)} %bitcast.15), channel_id=1, source_target_pairs={{0,16},{16,0},{1,17},{17,1},{2,18},{18,2},{3,19},{19,3},{4,20},{20... | collective-permute-start | bytes 20 | tf_op jit(solution)/shard_map/ppermute | solution.py:279
  134.0 38.3 %collective-permute-start.3 = (bf16[10,64,640]{2,1,0:T(8,128)(2,1)S(1)}, bf16[10,64,640]{2,1,0:T(8,128)(2,1)S(1)}, u32[]{:S(2)}, u32[]{:S(2)}) collective-permute-start(bf16[10,64,640]{2,1,0:T(8,128)(2,1)S(1)} %branch_1_fun.8), channel_id=1, source_target_pairs={{0,8},{1,9},{2,10},{3,11},{4,12},{5,13},{6,14},{7,15},{8,0},{9,1},... | collective-permute-start | bytes 2457608 | tf_op jit(solution)/shard_map/cond/branch_1_fun/ppermute | solution.py:307
  178.0 1.5 copy-start
  179.5 49.9 %all-to-all-start.3 = ((bf16[8,4,64,640]{3,2,1,0:T(8,128)(2,1)}), bf16[8,4,64,640]{3,2,1,0:T(8,128)(2,1)S(1)}, u32[]{:S(2)}, u32[]{:S(2)}) async-start(bf16[8,4,64,640]{3,2,1,0:T(8,128)(2,1)} %bitcast.71), calls=%async_computation.3 | async-start | bytes 5242880 | tf_op jit(solution)/shard_map/cond/branch_1_fun/all_to_all | solution.py:242
  183.2 43.2 %copy-start.14 = (bf16[24,64,512]{2,1,0:T(8,128)(2,1)S(1)}, bf16[24,64,512]{2,1,0:T(8,128)(2,1)}, u32[]{:S(2)}) copy-start(bf16[24,64,512]{2,1,0:T(8,128)(2,1)} %get-tuple-element.89.refs_0_) | copy-start | bytes 4718596 | tf_op jit(solution)/shard_map/cond
  185.1 41.3 %collective-permute-start.2 = (bf16[10,64,512]{2,1,0:T(8,128)(2,1)S(1)}, bf16[10,64,512]{2,1,0:T(8,128)(2,1)S(1)}, u32[]{:S(2)}, u32[]{:S(2)}) collective-permute-start(bf16[10,64,512]{2,1,0:T(8,128)(2,1)S(1)} %branch_1_fun.6), channel_id=1, source_target_pairs={{0,8},{1,9},{2,10},{3,11},{4,12},{5,13},{6,14},{7,15},{8,0},{9,1},... | collective-permute-start | bytes 1966088 | tf_op jit(solution)/shard_map/cond/branch_1_fun/ppermute | solution.py:307
  228.1 1.3 copy-start.6
  229.4 31.0 %all-to-all-start.2 = ((bf16[8,4,64,512]{3,2,1,0:T(8,128)(2,1)}), bf16[8,4,64,512]{3,2,1,0:T(8,128)(2,1)}, u32[]{:S(2)}, u32[]{:S(2)}) async-start(bf16[8,4,64,512]{3,2,1,0:T(8,128)(2,1)} %bitcast.77), calls=%async_computation.2 | async-start | bytes 4194304 | tf_op jit(solution)/shard_map/cond/branch_1_fun/all_to_all | solution.py:242

commit v3 on v1

--- a/solution.py
+++ b/solution.py
@@ -42,33 +42,22 @@
     )(slot_of, parts)
 
 
-def low_kernel(lane_groups, fill_ref, parts_ref, grad_ref, out_ref, weight):
+def rank_kernel(lane_groups, fill_ref, parts_ref, low_ref, grad_ref, out_ref, weight):
     parts, blocks, rows, lanes = parts_ref.shape
+    copies, width = out_ref.shape[0], out_ref.shape[-1]
     for b in range(blocks):
         for p in range(parts):
             g, l = p // lane_groups, p % lane_groups
             weight[b, g * rows : (g + 1) * rows, l * lanes : (l + 1) * lanes] = parts_ref[p, b]
     for b in range(blocks):
-        low = SCALE * lax.dot_general(
-            weight[b],
-            grad_ref[b * BLOCK : (b + 1) * BLOCK, :],
-            (((1,), (1,)), ((), ())),
-            preferred_element_type=F32,
+        grad = grad_ref[b * BLOCK : (b + 1) * BLOCK, :]
+        turned = SCALE * lax.dot_general(
+            weight[b], grad, (((1,), (1,)), ((), ())), preferred_element_type=F32
         )
-        live = lax.broadcasted_iota(jnp.int32, low.shape, 1) < fill_ref[b]
-        out_ref[b] = jnp.where(live, low, 0.0).astype(BF16)
-
-
-def rank_cotangent(fill, parts, grad, lane_groups, rank):
-    blocks = fill.shape[0]
-    return pl.pallas_call(
-        functools.partial(low_kernel, lane_groups),
-        out_shape=jax.ShapeDtypeStruct((blocks, rank, BLOCK), BF16),
-        in_specs=[pl.BlockSpec(memory_space=pltpu.SMEM), spec(), spec()],
-        out_specs=spec(),
-        scratch_shapes=[pltpu.VMEM((blocks, rank, grad.shape[1]), BF16)],
-        compiler_params=params(),
-    )(fill, parts, grad)
+        live = lax.broadcasted_iota(jnp.int32, turned.shape, 1) < fill_ref[b]
+        turned = jnp.where(live, turned, 0.0).astype(BF16)
+        for d in range(copies):
+            out_ref[d, b] = turned
 
 
 def up_kernel(fill_ref, low_ref, grad_ref, out_ref):
@@ -84,6 +73,26 @@
             out_ref[p, b] = whole[:, p * width : (p + 1) * width].astype(BF16)
 
 
+def rank_and_up_kernel(lane_groups, fill_ref, parts_ref, low_ref, grad_ref, out_ref, weight):
+    rank_kernel(lane_groups, fill_ref, parts_ref, low_ref, grad_ref, out_ref, weight)
+    blocks = fill_ref.shape[0]
+    up_kernel(fill_ref, low_ref, grad_ref, out_ref.at[:, blocks:])
+
+
+def rank_cotangent(fill, parts, low_t, grad, lane_groups, copies, with_up):
+    blocks, rank = fill.shape[0], low_t.shape[0]
+    return pl.pallas_call(
+        functools.partial(rank_and_up_kernel if with_up else rank_kernel, lane_groups),
+        out_shape=jax.ShapeDtypeStruct(
+            (copies, (2 if with_up else 1) * blocks, rank, BLOCK), BF16
+        ),
+        in_specs=[pl.BlockSpec(memory_space=pltpu.SMEM), spec(), spec(), spec()],
+        out_specs=spec(),
+        scratch_shapes=[pltpu.VMEM((blocks, rank, grad.shape[1]), BF16)],
+        compiler_params=params(),
+    )(fill, parts, low_t, grad)
+
+
 def up_products(fill, low_t, grad, parts):
     blocks, rank = fill.shape[0], low_t.shape[0]
     return pl.pallas_call(
@@ -96,21 +105,21 @@
 
 
 def down_kernel(low_ref, acts_ref, out_ref):
-    for b in range(low_ref.shape[0]):
+    for b in range(out_ref.shape[1]):
         out_ref[0, b] = jnp.dot(
-            low_ref[b], acts_ref[b * BLOCK : (b + 1) * BLOCK, :], preferred_element_type=F32
+            low_ref[0, b], acts_ref[b * BLOCK : (b + 1) * BLOCK, :], preferred_element_type=F32
         ).astype(BF16)
 
 
 def down_products(low_t, acts, parts, chunk):
-    blocks, rank, _ = low_t.shape
+    rank, blocks = low_t.shape[2], acts.shape[0] // BLOCK
     rows, width = acts.shape[0], acts.shape[1] // (parts * CHUNKS)
     return pl.pallas_call(
         down_kernel,
         grid=(parts,),
         out_shape=jax.ShapeDtypeStruct((parts, blocks, rank, width), BF16),
         in_specs=[
-            pl.BlockSpec(low_t.shape, lambda p: (0, 0, 0)),
+            pl.BlockSpec((1,) + low_t.shape[1:], lambda p: (0, 0, 0, 0)),
             pl.BlockSpec((rows, width), lambda p: (0, chunk * parts + p)),
         ],
         out_specs=pl.BlockSpec((1, blocks, rank, width), lambda p: (p, 0, 0, 0)),
@@ -123,54 +132,143 @@
     )(low_t, acts)
 
 
-def sum_kernel(blocks, targets, table_ref, held_ref, *refs):
-    extra_ref, out_ref = refs if len(refs) == 2 else (None, refs[0])
-    first, last = blocks, blocks + targets
+def extras(extra_ref, table_ref, at, until, low, high, total):
+    if extra_ref is None:
+        return total
+
+    def add(j, total):
+        return total + extra_ref[j, :, low:high].astype(F32)
+
+    return lax.fori_loop(table_ref[at], table_ref[until], add, total)
+
+
+def held_kernel(blocks, has_extra, table_ref, held_ref, *refs):
+    out_ref, extra_ref = refs[-1], refs[0] if has_extra else None
+    targets, rank, width = out_ref.shape
+    base = 3 * blocks
 
     def step(t, carry):
         def add(j, total):
             return total + held_ref[table_ref[j]].astype(F32)
 
         total = lax.fori_loop(
-            table_ref[first + t], table_ref[last + t], add, jnp.zeros(out_ref.shape[1:], F32)
+            table_ref[base + t],
+            table_ref[base + targets + t],
+            add,
+            jnp.zeros((rank, width), F32),
         )
-        if extra_ref is not None:
-            place = last + targets
-
-            def add_extra(j, total):
-                return total + extra_ref[j].astype(F32)
-
-            total = lax.fori_loop(
-                table_ref[place + t], table_ref[place + targets + t], add_extra, total
-            )
+        total = extras(
+            extra_ref,
+            table_ref,
+            base + 2 * targets + t,
+            base + 3 * targets + t,
+            0,
+            width,
+            total,
+        )
         out_ref[t] = total.astype(BF16)
         return carry
 
     lax.fori_loop(0, targets, step, 0)
 
 
-def slot_sums(table, held, targets, extra=None):
+def held_sums(table, held, targets, extra=None):
+    blocks, rank, width = held.shape
     operands = (held,) if extra is None else (held, extra)
-    size = held.shape[1] * held.shape[2]
-    moved = 2 * size * (targets + sum(x.shape[0] for x in operands))
-    return pl.pallas_call(
-        functools.partial(sum_kernel, held.shape[0], targets),
-        out_shape=jax.ShapeDtypeStruct((targets,) + held.shape[1:], BF16),
+    return pl.pallas_call(
+        functools.partial(held_kernel, blocks, extra is not None),
+        out_shape=jax.ShapeDtypeStruct((targets, rank, width), BF16),
         in_specs=[pl.BlockSpec(memory_space=pltpu.SMEM)] + [spec()] * len(operands),
         out_specs=spec(),
         compiler_params=params(),
         cost_estimate=pl.CostEstimate(
-            flops=size * held.shape[0], bytes_accessed=moved, transcendentals=0
+            flops=rank * width * blocks,
+            bytes_accessed=2 * targets * rank * width + 2 * sum(x.size for x in operands),
+            transcendentals=0,
         ),
     )(table, *operands)
 
 
+def taken_kernel(blocks, has_extra, parts, has_up, table_ref, low_ref, *refs):
+    up_ref, refs = (refs[0], refs[1:]) if has_up else (low_ref, refs)
+    up_order, up_shift = (0, 0) if has_up else (blocks, blocks // parts)
+    pieces, refs = refs[:parts], refs[parts:]
+    extra_ref = refs[0] if has_extra else None
+    out_ref, rows, sems = refs[-3:]
+    each = blocks // parts
+    copies = [
+        pltpu.make_async_copy(piece, rows.at[pl.ds(k * each, each)], sems.at[k])
+        for k, piece in enumerate(pieces)
+    ]
+    for copy in copies:
+        copy.start()
+    targets, rank, whole = out_ref.shape
+    width = rows.shape[2]
+    base = 3 * blocks
+    for copy in copies:
+        copy.wait()
+
+    def step(t, carry):
+        begin, end = table_ref[base + t], table_ref[base + targets + t]
+        at, until = base + 2 * targets + t, base + 3 * targets + t
+
+        def add(j, total):
+            return total + up_ref[table_ref[up_order + j] + up_shift].astype(F32)
+
+        total = lax.fori_loop(begin, end, add, jnp.zeros((rank, whole - width), F32))
+        total = extras(extra_ref, table_ref, at, until, width, whole, total)
+        out_ref[t, :, width:] = total.astype(BF16)
+
+        def multiply(j, total):
+            return total + jnp.dot(
+                low_ref[table_ref[blocks + j]],
+                rows[table_ref[2 * blocks + j]],
+                preferred_element_type=F32,
+            )
+
+        total = lax.fori_loop(begin, end, multiply, jnp.zeros((rank, width), F32))
+        total = extras(extra_ref, table_ref, at, until, 0, width, total)
+        out_ref[t, :, :width] = total.astype(BF16)
+        return carry
+
+    lax.fori_loop(0, targets, step, 0)
+
+
+def taken_sums(table, low, up, pieces, targets, extra=None, after=None):
+    rank, parts, width = low.shape[1], len(pieces), pieces[0].shape[2]
+    blocks = parts * pieces[0].shape[0]
+    whole = width + (low if up is None else up).shape[2]
+    vmem, anywhere = spec(), pl.BlockSpec(memory_space=pl.ANY)
+    operands = [table, low] + ([] if up is None else [up]) + [*pieces]
+    specs = [pl.BlockSpec(memory_space=pltpu.SMEM)] + [vmem] * (len(operands) - 1 - parts)
+    specs += [anywhere] * parts
+    if extra is not None:
+        operands += [extra, after]
+        specs += [vmem, anywhere]
+    return pl.pallas_call(
+        functools.partial(taken_kernel, blocks, extra is not None, parts, up is not None),
+        out_shape=jax.ShapeDtypeStruct((targets, rank, whole), BF16),
+        in_specs=specs,
+        out_specs=vmem,
+        scratch_shapes=[
+            pltpu.VMEM((blocks, BLOCK, width), BF16),
+            pltpu.SemaphoreType.DMA((parts,)),
+        ],
+        compiler_params=params(),
+        cost_estimate=pl.CostEstimate(
+            flops=2 * BLOCK * rank * whole * blocks,
+            bytes_accessed=2 * targets * rank * whole + 2 * sum(x.size for x in operands[1:]),
+            transcendentals=0,
+        ),
+    )(*operands)
+
+
 def place_kernel(got_ref, *refs):
     refs[-1][...] = got_ref[0]
 
 
-def place(got, columns, chunk, into=None):
-    parts, slots, rank, width = got.shape
+def place(got, width, columns, chunk, into=None):
+    parts, slots, rank, _ = got.shape
     return pl.pallas_call(
         place_kernel,
         grid=(parts,),
@@ -186,7 +284,7 @@
     )(*((got,) if into is None else (got, into)))
 
 
-def body(devices, acts, grad_out, low_acts, up_weight, block_adapter, block_fill, owner_slot):
+def body(copies, devices, acts, grad_out, low_acts, up_weight, block_adapter, block_fill, owner_slot):
     own_blocks = block_fill.shape[0]
     blocks, adapters = block_adapter.shape[0], owner_slot.shape[0]
     own_slots, rank, out_width = up_weight.shape
@@ -214,8 +312,14 @@
     picked = pick(slot_of, part).reshape(devices, own_blocks, rows, lanes)
     weights = lax.all_to_all(picked, "dp", 0, 0, tiled=True)
 
-    up_held = within(up_products(block_fill, low_acts.T, grad_out, half_devices))
-    up_held = up_held.reshape(half_blocks, rank, -1)
+    place_in_half = lax.axis_index("dp") % half_devices
+    width = model_width // (CHUNKS * half_devices)
+    pieces = []
+    for k in range(half_devices):
+        piece = lax.dynamic_slice_in_dim(acts, (place_in_half ^ k) * width, width, axis=1)
+        if k:
+            piece = lax.ppermute(piece, "dp", [(i, i ^ k) for i in range(devices)])
+        pieces.append(piece.reshape(own_blocks, BLOCK, width))
 
     mine = lax.dynamic_slice_in_dim(slot_of, half * half_blocks, half_blocks)
     spots = jnp.arange(half_blocks, dtype=jnp.int32)
@@ -224,6 +328,15 @@
     )
     spot_of = jnp.sum(before.astype(jnp.int32), axis=1)
     order = jnp.sum(jnp.where(spot_of[None, :] == spots[:, None], spots[None, :], 0), axis=1)
+    source, spot = order // own_blocks, order % own_blocks
+    with_up = out_width // half_devices == BLOCK
+    order = jnp.concatenate(
+        [
+            order,
+            (2 if with_up else 1) * own_blocks * source + spot,
+            (source ^ place_in_half) * own_blocks + spot,
+        ]
+    )
     start = jnp.sum((mine[None, :] < ids[:, None]).astype(jnp.int32), axis=1)
     count = jnp.sum((mine[None, :] == ids[:, None]).astype(jnp.int32), axis=1)
     by_half = slot_of.reshape(2, half_blocks)
@@ -231,7 +344,12 @@
     crosses = has & ((ids[None, :] // half_slots) != jnp.arange(2, dtype=jnp.int32)[:, None])
     earlier = (ids[None, :] < ids[:, None])[None, :, :]
     place_of = jnp.sum((crosses[:, None, :] & earlier).astype(jnp.int32), axis=2)
-    needed = lax.pmax(jnp.max(jnp.sum(crosses.astype(jnp.int32), axis=1)), "groups")
+    mine_needed = jnp.max(jnp.sum(crosses.astype(jnp.int32), axis=1)).reshape(1, 1)
+    needed = mine_needed
+    for k in range(1, copies):
+        shift = [(i, (i + k) % copies) for i in range(copies)]
+        needed = jnp.maximum(needed, lax.ppermute(mine_needed, "groups", shift))
+    needed = needed[0, 0]
 
     my_cross = lax.dynamic_index_in_dim(crosses, half, 0, False)
     my_place = lax.dynamic_index_in_dim(place_of, half, 0, False)
@@ -248,36 +366,40 @@
     got_first = lax.dynamic_slice_in_dim(got_first, own, half_slots)
     keep_table = jnp.concatenate([order, keep_first, keep_last, got_first, got_first + got])
 
-    low_t = rank_cotangent(block_fill, weights, grad_out, lane_groups, rank)
-
-    def rest(capacity, acts, low_t, up_held, order, send_first, send_last, keep_table):
+    low_t = rank_cotangent(
+        block_fill, weights, low_acts.T, grad_out, lane_groups, half_devices, with_up
+    )
+    low = within(low_t).reshape(-1, rank, BLOCK)
+    up_held = ()
+    if not with_up:
+        up_held = within(up_products(block_fill, low_acts.T, grad_out, half_devices))
+        up_held = (up_held.reshape(half_blocks, rank, -1),)
+    products = down_products(low_t, acts, half_devices, 1)
+
+    def rest(capacity, low, up_held, products, order, send_first, send_last, keep_table, *pieces):
+        up_held = up_held[0] if up_held else None
         send_table = jnp.concatenate([order, send_first[:capacity], send_last[:capacity]])
-
-        def finish(held):
-            crossing = slot_sums(send_table, held, capacity)
-            arrived = lax.ppermute(crossing, "dp", across)
-            kept = slot_sums(keep_table, held, half_slots, arrived)
-            return within(kept.reshape(half_devices, own_slots, rank, -1))
-
-        held = [
-            within(down_products(low_t, acts, half_devices, c)).reshape(half_blocks, rank, -1)
-            for c in range(CHUNKS)
-        ]
-        up = place(finish(up_held), out_width, 0) if out_width // half_devices >= 128 else (
-            finish(up_held).transpose(1, 2, 0, 3).reshape(own_slots, rank, out_width)
-        )
-        down = None
-        for c in range(CHUNKS):
-            down = place(finish(held[c]), model_width, c, down)
+        held = within(products).reshape(half_blocks, rank, -1)
+        sent_a = taken_sums(send_table, low, up_held, pieces, capacity)
+        came_a = lax.ppermute(sent_a, "dp", across)
+        sent_b = held_sums(send_table, held, capacity)
+        came_b = lax.ppermute(sent_b, "dp", across)
+        kept_a = taken_sums(keep_table, low, up_held, pieces, half_slots, came_a, sent_b)
+        first = within(kept_a.reshape(half_devices, own_slots, rank, -1))
+        kept_b = held_sums(keep_table, held, half_slots, came_b)
+        second = within(kept_b.reshape(half_devices, own_slots, rank, -1))
+        up = first[:, :, :, width:].transpose(1, 2, 0, 3).reshape(own_slots, rank, out_width)
+        down = place(first, width, model_width, 0)
+        down = place(second, width, model_width, 1, down)
         return down, up
 
     limit = min(half_blocks, half_slots)
-    capacities = sorted({-(-limit * k // 24) for k in (8, 10, 12, 16, 24)})
+    capacities = sorted({-(-limit * k // 24) for k in (8, 9, 10, 11, 12, 14, 16, 24)})
     index = sum((needed > c).astype(jnp.int32) for c in capacities[:-1])
     return lax.switch(
         index,
         [functools.partial(rest, c) for c in capacities],
-        acts, low_t, up_held, order, send_first, send_last, keep_table,
+        low, up_held, products, order, send_first, send_last, keep_table, *pieces,
     )
 
 
@@ -292,7 +414,7 @@
         P(),
     )
     return jax.shard_map(
-        functools.partial(body, mesh.shape["dp"]),
+        functools.partial(body, mesh.shape["groups"], mesh.shape["dp"]),
         mesh=mesh,
         in_specs=placed,
         out_specs=(P(("groups", "dp"), None, None), P(("groups", "dp"), None, None)),

time: 222 us -> 216 us (0.973); the launches traced: 224 us -> 215 us
  blocking collectives: 4.89 us -> 0 us
  local copies, waits for them, and re-layouts: 6.53 us -> 10.8 us
  waiting for transfers between devices: 130 us -> 126 us
  Pallas kernels: 35 us -> 31.3 us
    all_to_all x6 -> x4, waiting for transfers between devices: 33.5 us -> 44.3 us  [within(): return lax.all_to_all(x, 'dp', 0, 0, axis_index_groups=groups, tiled=True)]
    all_to_all x6 -> x4, starting transfers between devices: 26.3 us -> 17.4 us  [within(): return lax.all_to_all(x, 'dp', 0, 0, axis_index_groups=groups, tiled=True)]
    all_to_all x1, waiting for transfers between devices: 9.55 us -> 1.96 us  [body(): weights = lax.all_to_all(picked, 'dp', 0, 0, tiled=True)]
    ppermute x3 -> x10, starting transfers between devices: 5.18 us -> 12.2 us  [the longest x7 7.77 us: body(): piece = lax.ppermute(piece, 'dp', [(i, i ^ k) for i in range(devices)])]
    ppermute x3 -> x10, waiting for transfers between devices: 72.5 us -> 65.8 us  [the longest x1 38.9 us: rest(): came_b = lax.ppermute(sent_b, 'dp', across)]
    pallas_call x2 -> x1, Pallas kernels: 11.5 us -> 6.42 us  [down_products(): pl.pallas_call(down_kernel, grid=(parts,), out_shape=jax.ShapeDtypeStruct...]
    pmax x1 -> x0, blocking collectives: 4.89 us -> none  [body(): lax.pmax(jnp.max(jnp.sum(crosses.astype(jnp.int32), axis=1)), 'groups')]
    pallas_call x8 -> x5, Pallas kernels: 10.7 us -> 14.7 us  [the longest x2 10.3 us: taken_sums(): pl.pallas_call(functools.partial(taken_kernel, blocks, extra is not None,...]
  transfers between devices with their start and end apart: 11 -> 16, of which waited for: 8 -> 9; matrix products, arithmetic and copies ran while one was open for 1% -> 4% of each run, Pallas kernels for 12% -> 10%
where the time goes in v3:
time: 216 us; the launch traced here: 215 us
  waiting for transfers between devices  126 us (58%)
  starting transfers between devices  41.1 us (19%)
  Pallas kernels  31.3 us (14%)
  local copies, waits for them, and re-layouts  10.8 us (5%)
  other arithmetic  3.06 us (1%)
    all_to_all x4, waiting for transfers between devices, within(): return lax.all_to_all(x, 'dp', 0, 0, axis_index_groups=groups, tiled=True)  44.3 us
    ppermute x1, waiting for transfers between devices, rest(): came_b = lax.ppermute(sent_b, 'dp', across)  38.9 us
    ppermute x7, waiting for transfers between devices, body(): piece = lax.ppermute(piece, 'dp', [(i, i ^ k) for i in range(devices)])  23.3 us
    all_to_all x4, starting transfers between devices, within(): return lax.all_to_all(x, 'dp', 0, 0, axis_index_groups=groups, tiled=True)  17.4 us
    all_to_all x1, waiting for transfers between devices, body(): lax.all_to_all(pieces, 'dp', 0, 0, tiled=True)  14.1 us
    pallas_call x2, Pallas kernels, taken_sums(): pl.pallas_call(functools.partial(taken_kernel, blocks, extra is not None,...  10.3 us
    pallas_call x2, Pallas kernels, place(): pl.pallas_call(place_kernel, grid=(parts,), out_shape=jax.ShapeDtypeStruc...  8.59 us
    ppermute x7, starting transfers between devices, body(): piece = lax.ppermute(piece, 'dp', [(i, i ^ k) for i in range(devices)])  7.77 us
  transfers between devices with their start and end apart: 16, of which 9 were waited for; matrix products, arithmetic and copies ran while one was open for 4% of the time, Pallas kernels for 10%

profile of v3, /device:TPU:0, one launch (start us, length us, event | category | flops | bytes accessed | tf_op | source)
XLA Modules:
  0.0 214.6 jit_solution(5131077410050249786)
XLA Ops:
  3.0 7.4 %all-to-all-start.24 = ((bf16[16,4,16,256]{3,2,1,0:T(8,128)(2,1)}), bf16[16,4,16,256]{3,2,1,0:T(8,128)(2,1)S(1)}, u32[]{:S(2)}, u32[]{:S(2)}) async-start(bf16[16,4,16,256]{3,2,1,0:T(8,128)(2,1)} %bitcast.35), calls=%async_computation.24 | async-start | bytes 1048576 | tf_op jit(solution)/shard_map/all_to_all | solution.py:311
  10.8 14.1 %all-to-all-done.24 = bf16[16,4,16,256]{3,2,1,0:T(8,128)(2,1)S(1)} async-done(((bf16[16,4,16,256]{3,2,1,0:T(8,128)(2,1)}), bf16[16,4,16,256]{3,2,1,0:T(8,128)(2,1)S(1)}, u32[]{:S(2)}, u32[]{:S(2)}) %all-to-all-start.24) | async-done | bytes 524320 | tf_op jit(solution)/shard_map/all_to_all | solution.py:311
  26.4 4.1 %all-to-all-start.25 = ((bf16[16,3,16,256]{3,2,1,0:T(8,128)(2,1)}), bf16[16,3,16,256]{3,2,1,0:T(8,128)(2,1)S(1)}, u32[]{:S(2)}, u32[]{:S(2)}) async-start(bf16[16,3,16,256]{3,2,1,0:T(8,128)(2,1)} %bitcast.37), calls=%async_computation.25 | async-start | bytes 786432 | tf_op jit(solution)/shard_map/all_to_all | solution.py:313
  32.8 3.3 %constant_dynamic-slice_fusion.9 = (bf16[384,512]{1,0:T(8,128)(2,1)}, bf16[384,512]{1,0:T(8,128)(2,1)}, bf16[384,512]{1,0:T(8,128)(2,1)}, bf16[384,512]{1,0:T(8,...) fusion(bf16[384,8192]{1,0:T(8,128)(2,1)} %acts_ref.1, ...), kind=kLoop, calls=%fused_computation.53 | loop fusion | bytes 6291488 | tf_op jit(solution)/shard_map/dynamic_slice | solution.py:319
  36.1 2.3 %collective-permute-start.23 = (bf16[384,512]{1,0:T(8,128)(2,1)}, bf16[384,512]{1,0:T(8,128)(2,1)S(1)}, u32[]{:S(2)}, u32[]{:S(2)}) collective-permute-start(bf16[384,512]{1,0:T(8,128)(2,1)} %get-tuple-element.350), channel_id=1, source_target_pairs={{0,7},{1,6},{2,5},{3,4},{4,3},{5,2},{6,1},{7,0},{8,15},{9,14},{10,... | collective-permute-start | bytes 1179656 | tf_op jit(solution)/shard_map/ppermute | solution.py:321
  40.9 2.0 all-to-all-done.25.parts_ref
  44.8 3.5 %all-to-all-start.26 = ((bf16[8,6,64,128]{3,2,1,0:T(8,128)(2,1)}), bf16[8,6,64,128]{3,2,1,0:T(8,128)(2,1)S(1)}, u32[]{:S(2)}, u32[]{:S(2)}) async-start(bf16[8,6,64,128]{3,2,1,0:T(8,128)(2,1)} %shard_map.103.low_ref), calls=%async_computation.26 | async-start | bytes 1572864 | tf_op jit(solution)/shard_map/all_to_all | solution.py:299
  49.1 2.0 collective-permute-start.18
  51.1 7.4 %collective-permute-done.21 = bf16[384,512]{1,0:T(8,128)(2,1)} collective-permute-done((bf16[384,512]{1,0:T(8,128)(2,1)}, bf16[384,512]{1,0:T(8,128)(2,1)}, u32[]{:S(2)}, u32[]{:S(2)}) %collective-permute-start.21) | collective-permute-done | bytes 393248 | tf_op jit(solution)/shard_map/ppermute | solution.py:321
  61.7 6.4 %shard_map.104 = bf16[8,3,64,512]{3,2,1,0:T(8,128)(2,1)} custom-call(bf16[8,6,64,128]{3,2,1,0:T(8,128)(2,1)} %shard_map.103.low_ref, bf16[384,8192]{1,0:T(8,128)(2,1)} %acts_ref.1), custom_call_target="tpu_custom_call" | custom-call | flops 201326592 | bytes 4718592 | tf_op jit(solution)/shard_map/pallas_call | solution.py:117
  68.2 7.6 %collective-permute-done.18 = bf16[384,512]{1,0:T(8,128)(2,1)} collective-permute-done((bf16[384,512]{1,0:T(8,128)(2,1)}, bf16[384,512]{1,0:T(8,128)(2,1)}, u32[]{:S(2)}, u32[]{:S(2)}) %collective-permute-start.18) | collective-permute-done | bytes 393248 | tf_op jit(solution)/shard_map/ppermute | solution.py:321
  75.8 8.3 %collective-permute-done.22 = bf16[384,512]{1,0:T(8,128)(2,1)} collective-permute-done((bf16[384,512]{1,0:T(8,128)(2,1)S(1)}, bf16[384,512]{1,0:T(8,128)(2,1)}, u32[]{:S(2)}, u32[]{:S(2)}) %collective-permute-start.22) | collective-permute-done | bytes 393248 | tf_op jit(solution)/shard_map/ppermute | solution.py:321
  84.1 130.5 %conditional.1 = (bf16[4,64,8192]{2,1,0:T(8,128)(2,1)}, bf16[4,64,1024]{2,1,0:T(8,128)(2,1)}) conditional(s32[]{:T(128)} %bitcast.33, (bf16[8,3,64,512]{3,2,1,0:T(8,128)(2,1)}, s32[24]{0:T(128)}, s32[24]{0:T(128)S(1)}, s32[72]{0:T(128)S(1)}, s32[200]{0:T(256)S(1)}, /*index=5*/bf16[48,64,128]{2,1,0:T(8,128)(2,1)S(1)}, ...), branch_computations={%region_11.12_spmd, %region_12.13_spmd, %region_13.14_spmd, %regio... | conditional | flops 504889600 | bytes 99878264 | solution.py:399
  84.1 3.6 %all-to-all-start = ((bf16[8,3,64,512]{3,2,1,0:T(8,128)(2,1)}), bf16[8,3,64,512]{3,2,1,0:T(8,128)(2,1)S(1)}, u32[]{:S(2)}, u32[]{:S(2)}) async-start(bf16[8,3,64,512]{3,2,1,0:T(8,128)(2,1)} %get-tuple-element.225), calls=%async_computation | async-start | bytes 3145728 | tf_op jit(solution)/shard_map/cond/branch_0_fun/all_to_all | solution.py:299
  88.4 4.3 %branch_0_fun.8 = bf16[8,64,640]{2,1,0:T(8,128)(2,1)S(1)} custom-call(s32[88]{0:T(128)S(1)} %pad_add_fusion.table_ref, bf16[48,64,128]{2,1,0:T(8,128)(2,1)S(1)} %get-tuple-element.229.low_ref, bf16[3,128,512]{2,1,0:T(8,128)(2,1)S(1)} %get-tuple-element.230.refs_0_, bf16[3,128,512]{2,1,0:T(8,128)(2,1)} %get-tuple-element.231.refs_1_, ...), custom_call_target="tpu_custom_call" | custom-call | flops 251658240 | bytes 4587520 | tf_op jit(solution)/shard_map/cond/branch_0_fun/pallas_call | solution.py:248
  94.1 26.2 %all-to-all-done = bf16[8,3,64,512]{3,2,1,0:T(8,128)(2,1)S(1)} async-done(((bf16[8,3,64,512]{3,2,1,0:T(8,128)(2,1)}), bf16[8,3,64,512]{3,2,1,0:T(8,128)(2,1)S(1)}, u32[]{:S(2)}, u32[]{:S(2)}) %all-to-all-start) | async-done | bytes 1572896 | tf_op jit(solution)/shard_map/cond/branch_0_fun/all_to_all | solution.py:299
  121.2 3.6 %collective-permute-done.1.refs_8_ = bf16[8,64,640]{2,1,0:T(8,128)(2,1)S(1)} collective-permute-done((bf16[8,64,640]{2,1,0:T(8,128)(2,1)S(1)}, bf16[8,64,640]{2,1,0:T(8,128)(2,1)S(1)}, u32[]{:S(2)}, u32[]{:S(2)}) %collective-permute-start.1) | collective-permute-done | bytes 655392 | tf_op jit(solution)/shard_map/cond/branch_0_fun/ppermute | solution.py:384
  124.8 6.0 %branch_0_fun.9 = bf16[32,64,640]{2,1,0:T(8,128)(2,1)S(1)} custom-call(s32[200]{0:T(256)S(1)} %get-tuple-element.224.table_ref, bf16[48,64,128]{2,1,0:T(8,128)(2,1)S(1)} %copy-done.20, bf16[3,128,512]{2,1,0:T(8,128)(2,1)} %copy-done.35, bf16[3,128,512]{2,1,0:T(8,128)(2,1)} %get-tuple-element.231.refs_1_, bf16[3,128,512]{2,1,0:T(8,128)(2,1)} %get-tuple-element.232.refs_2_, ...), custom_call_target="tpu_custom_call" | custom-call | flops 251658240 | bytes 7733248 | tf_op jit(solution)/shard_map/cond/branch_0_fun/pallas_call | solution.py:248
  132.3 4.4 %all-to-all-start.2 = ((bf16[8,4,64,640]{3,2,1,0:T(8,128)(2,1)}), bf16[8,4,64,640]{3,2,1,0:T(8,128)(2,1)}, u32[]{:S(2)}, u32[]{:S(2)}) async-start(bf16[8,4,64,640]{3,2,1,0:T(8,128)(2,1)} %bitcast.131), calls=%async_computation.2 | async-start | bytes 5242880 | tf_op jit(solution)/shard_map/cond/branch_0_fun/all_to_all | solution.py:299
  138.2 38.9 %collective-permute-done.refs_0_ = bf16[8,64,512]{2,1,0:T(8,128)(2,1)S(1)} collective-permute-done((bf16[8,64,512]{2,1,0:T(8,128)(2,1)S(1)}, bf16[8,64,512]{2,1,0:T(8,128)(2,1)S(1)}, u32[]{:S(2)}, u32[]{:S(2)}) %collective-permute-start) | collective-permute-done | bytes 524320 | tf_op jit(solution)/shard_map/cond/branch_0_fun/ppermute | solution.py:386
  180.1 5.9 %all-to-all-start.1 = ((bf16[8,4,64,512]{3,2,1,0:T(8,128)(2,1)}), bf16[8,4,64,512]{3,2,1,0:T(8,128)(2,1)S(1)}, u32[]{:S(2)}, u32[]{:S(2)}) async-start(bf16[8,4,64,512]{3,2,1,0:T(8,128)(2,1)} %bitcast.138), calls=%async_computation.1 | async-start | bytes 4194304 | tf_op jit(solution)/shard_map/cond/branch_0_fun/all_to_all | solution.py:299
  186.0 5.6 %branch_0_fun.10.refs_0_ = bf16[4,64,8192]{2,1,0:T(8,128)(2,1)} custom-call(bf16[8,4,64,640]{3,2,1,0:T(8,128)(2,1)} %all-to-all-done.2.got_ref), custom_call_target="tpu_custom_call" | custom-call | bytes 4194304 | tf_op jit(solution)/shard_map/cond/branch_0_fun/pallas_call | solution.py:272
  193.5 18.1 %all-to-all-done.1.got_ref = bf16[8,4,64,512]{3,2,1,0:T(8,128)(2,1)S(1)} async-done(((bf16[8,4,64,512]{3,2,1,0:T(8,128)(2,1)}), bf16[8,4,64,512]{3,2,1,0:T(8,128)(2,1)S(1)}, u32[]{:S(2)}, u32[]{:S(2)}) %all-to-all-start.1) | async-done | bytes 2097184 | tf_op jit(solution)/shard_map/cond/branch_0_fun/all_to_all | solution.py:299
  211.7 3.0 %branch_0_fun.11 = bf16[4,64,8192]{2,1,0:T(8,128)(2,1)} custom-call(bf16[8,4,64,512]{3,2,1,0:T(8,128)(2,1)S(1)} %all-to-all-done.1.got_ref, bf16[4,64,8192]{2,1,0:T(8,128)(2,1)} %branch_0_fun.10.refs_0_), custom_call_target="tpu_custom_call", output_to_operand_aliasing={{}: (1, {})} | custom-call | bytes 4194304 | tf_op jit(solution)/shard_map/cond/branch_0_fun/pallas_call | solution.py:272
  (68 shorter events, 24.5 us)
Async XLA Ops:
  0.6 9.7 %copy-start.62 = (s32[64]{0:T(128)S(1)}, s32[64]{0:T(128)}, u32[]{:S(2)}) copy-start(s32[64]{0:T(128)} %param.21) | copy-start | bytes 772
  0.6 9.7 %copy-start.63 = (s32[48]{0:T(128)S(1)}, s32[48]{0:T(128)}, u32[]{:S(2)}) copy-start(s32[48]{0:T(128)} %param.19) | copy-start | bytes 580
  3.0 21.9 %all-to-all-start.24 = ((bf16[16,4,16,256]{3,2,1,0:T(8,128)(2,1)}), bf16[16,4,16,256]{3,2,1,0:T(8,128)(2,1)S(1)}, u32[]{:S(2)}, u32[]{:S(2)}) async-start(bf16[16,4,16,256]{3,2,1,0:T(8,128)(2,1)} %bitcast.35), calls=%async_computation.24 | async-start | bytes 1048576 | tf_op jit(solution)/shard_map/all_to_all | solution.py:311
  26.4 16.5 %all-to-all-start.25 = ((bf16[16,3,16,256]{3,2,1,0:T(8,128)(2,1)}), bf16[16,3,16,256]{3,2,1,0:T(8,128)(2,1)S(1)}, u32[]{:S(2)}, u32[]{:S(2)}) async-start(bf16[16,3,16,256]{3,2,1,0:T(8,128)(2,1)} %bitcast.37), calls=%async_computation.25 | async-start | bytes 786432 | tf_op jit(solution)/shard_map/all_to_all | solution.py:313
  31.3 17.8 %collective-permute-start.16 = (s32[1,1]{1,0:T(1,128)}, s32[1,1]{1,0:T(1,128)}, u32[]{:S(2)}, u32[]{:S(2)}) collective-permute-start(s32[1,1]{1,0:T(1,128)} %bitcast.32), channel_id=1, source_target_pairs={{0,16},{16,0},{1,17},{17,1},{2,18},{18,2},{3,19},{19,3},{4,20},{20... | collective-permute-start | bytes 20 | tf_op jit(solution)/shard_map/ppermute | solution.py:351
  32.8 10.1 %copy-start.16 = (bf16[384,1024]{1,0:T(8,128)(2,1)S(1)}, bf16[384,1024]{1,0:T(8,128)(2,1)}, u32[]{:S(2)}) copy-start(bf16[384,1024]{1,0:T(8,128)(2,1)} %grad_ref.1) | copy-start | bytes 2359300
  32.8 10.1 %copy-start.17 = (bf16[384,64]{0,1:T(8,128)(2,1)S(1)}, bf16[384,64]{0,1:T(8,128)(2,1)}, u32[]{:S(2)}) copy-start(bf16[384,64]{0,1:T(8,128)(2,1)} %param.17) | copy-start | bytes 147460
  32.8 10.1 %copy-start.18 = (s32[3]{0:T(128)S(1)}, s32[3]{0:T(128)}, u32[]{:S(2)}) copy-start(s32[3]{0:T(128)} %fill_ref.1) | copy-start | bytes 40
  36.1 14.9 %collective-permute-start.23 = (bf16[384,512]{1,0:T(8,128)(2,1)}, bf16[384,512]{1,0:T(8,128)(2,1)S(1)}, u32[]{:S(2)}, u32[]{:S(2)}) collective-permute-start(bf16[384,512]{1,0:T(8,128)(2,1)} %get-tuple-element.350), channel_id=1, source_target_pairs={{0,7},{1,6},{2,5},{3,4},{4,3},{5,2},{6,1},{7,0},{8,15},{9,14},{10,... | collective-permute-start | bytes 1179656 | tf_op jit(solution)/shard_map/ppermute | solution.py:321
  38.4 20.0 %collective-permute-start.21 = (bf16[384,512]{1,0:T(8,128)(2,1)}, bf16[384,512]{1,0:T(8,128)(2,1)}, u32[]{:S(2)}, u32[]{:S(2)}) collective-permute-start(bf16[384,512]{1,0:T(8,128)(2,1)} %get-tuple-element.351), channel_id=1, source_target_pairs={{0,5},{1,4},{2,7},{3,6},{4,1},{5,0},{6,3},{7,2},{8,13},{9,12},{10,... | collective-permute-start | bytes 1179656 | tf_op jit(solution)/shard_map/ppermute | solution.py:321
  39.3 28.9 %collective-permute-start.20 = (bf16[384,512]{1,0:T(8,128)(2,1)}, bf16[384,512]{1,0:T(8,128)(2,1)}, u32[]{:S(2)}, u32[]{:S(2)}) collective-permute-start(bf16[384,512]{1,0:T(8,128)(2,1)} %get-tuple-element.352), channel_id=1, source_target_pairs={{0,4},{1,5},{2,6},{3,7},{4,0},{5,1},{6,2},{7,3},{8,12},{9,13},{10,... | collective-permute-start | bytes 1179656 | tf_op jit(solution)/shard_map/ppermute | solution.py:321
  40.7 27.4 %collective-permute-start.19 = (bf16[384,512]{1,0:T(8,128)(2,1)}, bf16[384,512]{1,0:T(8,128)(2,1)}, u32[]{:S(2)}, u32[]{:S(2)}) collective-permute-start(bf16[384,512]{1,0:T(8,128)(2,1)} %get-tuple-element.353), channel_id=1, source_target_pairs={{0,3},{1,2},{2,1},{3,0},{4,7},{5,6},{6,5},{7,4},{8,11},{9,10},{10,... | collective-permute-start | bytes 1179656 | tf_op jit(solution)/shard_map/ppermute | solution.py:321
  44.8 39.3 %all-to-all-start.26 = ((bf16[8,6,64,128]{3,2,1,0:T(8,128)(2,1)}), bf16[8,6,64,128]{3,2,1,0:T(8,128)(2,1)S(1)}, u32[]{:S(2)}, u32[]{:S(2)}) async-start(bf16[8,6,64,128]{3,2,1,0:T(8,128)(2,1)} %shard_map.103.low_ref), calls=%async_computation.26 | async-start | bytes 1572864 | tf_op jit(solution)/shard_map/all_to_all | solution.py:299
  49.1 26.7 %collective-permute-start.18 = (bf16[384,512]{1,0:T(8,128)(2,1)}, bf16[384,512]{1,0:T(8,128)(2,1)}, u32[]{:S(2)}, u32[]{:S(2)}) collective-permute-start(bf16[384,512]{1,0:T(8,128)(2,1)} %get-tuple-element.354), channel_id=1, source_target_pairs={{0,2},{1,3},{2,0},{3,1},{4,6},{5,7},{6,4},{7,5},{8,10},{9,11},{10,... | collective-permute-start | bytes 1179656 | tf_op jit(solution)/shard_map/ppermute | solution.py:321
  51.1 24.7 %collective-permute-start.17 = (bf16[384,512]{1,0:T(8,128)(2,1)}, bf16[384,512]{1,0:T(8,128)(2,1)}, u32[]{:S(2)}, u32[]{:S(2)}) collective-permute-start(bf16[384,512]{1,0:T(8,128)(2,1)} %get-tuple-element.355), channel_id=1, source_target_pairs={{0,1},{1,0},{2,3},{3,2},{4,5},{5,4},{6,7},{7,6},{8,9},{9,8},{10,11... | collective-permute-start | bytes 1179656 | tf_op jit(solution)/shard_map/ppermute | solution.py:321
  58.4 25.7 %collective-permute-start.22 = (bf16[384,512]{1,0:T(8,128)(2,1)S(1)}, bf16[384,512]{1,0:T(8,128)(2,1)}, u32[]{:S(2)}, u32[]{:S(2)}) collective-permute-start(bf16[384,512]{1,0:T(8,128)(2,1)S(1)} %get-tuple-element.357), channel_id=1, source_target_pairs={{0,6},{1,7},{2,4},{3,5},{4,2},{5,3},{6,0},{7,1},{8,14},{9,15},{10,... | collective-permute-start | bytes 1179656 | tf_op jit(solution)/shard_map/ppermute | solution.py:321
  84.1 4.3 %copy-start.46 = (bf16[3,128,512]{2,1,0:T(8,128)(2,1)}, bf16[3,128,512]{2,1,0:T(8,128)(2,1)S(1)}, u32[]{:S(2)}) copy-start(bf16[3,128,512]{2,1,0:T(8,128)(2,1)S(1)} %get-tuple-element.237.refs_7_) | copy-start | bytes 1179652 | tf_op jit(solution)/shard_map/cond
  84.1 4.3 %copy-start.19 = (bf16[48,64,128]{2,1,0:T(8,128)(2,1)}, bf16[48,64,128]{2,1,0:T(8,128)(2,1)S(1)}, u32[]{:S(2)}) copy-start(bf16[48,64,128]{2,1,0:T(8,128)(2,1)S(1)} %get-tuple-element.229.low_ref) | copy-start | bytes 2359300 | tf_op jit(solution)/shard_map/cond
  84.1 36.2 %all-to-all-start = ((bf16[8,3,64,512]{3,2,1,0:T(8,128)(2,1)}), bf16[8,3,64,512]{3,2,1,0:T(8,128)(2,1)S(1)}, u32[]{:S(2)}, u32[]{:S(2)}) async-start(bf16[8,3,64,512]{3,2,1,0:T(8,128)(2,1)} %get-tuple-element.225), calls=%async_computation | async-start | bytes 3145728 | tf_op jit(solution)/shard_map/cond/branch_0_fun/all_to_all | solution.py:299
  92.7 32.1 %collective-permute-start.1 = (bf16[8,64,640]{2,1,0:T(8,128)(2,1)S(1)}, bf16[8,64,640]{2,1,0:T(8,128)(2,1)S(1)}, u32[]{:S(2)}, u32[]{:S(2)}) collective-permute-start(bf16[8,64,640]{2,1,0:T(8,128)(2,1)S(1)} %branch_0_fun.8), channel_id=1, source_target_pairs={{0,8},{1,9},{2,10},{3,11},{4,12},{5,13},{6,14},{7,15},{8,0},{9,1},... | collective-permute-start | bytes 1966088 | tf_op jit(solution)/shard_map/cond/branch_0_fun/ppermute | solution.py:384
  120.3 4.5 %copy-start.20 = (bf16[48,64,128]{2,1,0:T(8,128)(2,1)S(1)}, bf16[48,64,128]{2,1,0:T(8,128)(2,1)}, u32[]{:S(2)}) copy-start(bf16[48,64,128]{2,1,0:T(8,128)(2,1)} %copy-done.19) | copy-start | bytes 2359300 | tf_op jit(solution)/shard_map/cond
  132.3 47.8 %all-to-all-start.2 = ((bf16[8,4,64,640]{3,2,1,0:T(8,128)(2,1)}), bf16[8,4,64,640]{3,2,1,0:T(8,128)(2,1)}, u32[]{:S(2)}, u32[]{:S(2)}) async-start(bf16[8,4,64,640]{3,2,1,0:T(8,128)(2,1)} %bitcast.131), calls=%async_computation.2 | async-start | bytes 5242880 | tf_op jit(solution)/shard_map/cond/branch_0_fun/all_to_all | solution.py:299
  136.7 40.4 %collective-permute-start = (bf16[8,64,512]{2,1,0:T(8,128)(2,1)S(1)}, bf16[8,64,512]{2,1,0:T(8,128)(2,1)S(1)}, u32[]{:S(2)}, u32[]{:S(2)}) collective-permute-start(bf16[8,64,512]{2,1,0:T(8,128)(2,1)S(1)} %branch_0_fun.6.refs_9_), channel_id=1, source_target_pairs={{0,8},{1,9},{2,10},{3,11},{4,12},{5,13},{6,14},{7,15},{8,0},{9,1},... | collective-permute-start | bytes 1572872 | tf_op jit(solution)/shard_map/cond/branch_0_fun/ppermute | solution.py:386
  180.1 31.6 %all-to-all-start.1 = ((bf16[8,4,64,512]{3,2,1,0:T(8,128)(2,1)}), bf16[8,4,64,512]{3,2,1,0:T(8,128)(2,1)S(1)}, u32[]{:S(2)}, u32[]{:S(2)}) async-start(bf16[8,4,64,512]{3,2,1,0:T(8,128)(2,1)} %bitcast.138), calls=%async_computation.1 | async-start | bytes 4194304 | tf_op jit(solution)/shard_map/cond/branch_0_fun/all_to_all | solution.py:299
  (3 other events, 7.1 us)
